TPU v7x, 128 devices: a whole 4x4x4 slice. The times are simulated.
128 devices in a mesh: ctx: 8 (over z, x_lo), exp: 16 (over y, x_hi, core).
Axes of the slice: x: 4 (x_hi: 2, x_lo: 2; x = x_hi * 2 + x_lo), y: 4, z: 4, core: 2. Of those that a mesh axis runs over, the one named last changes fastest.
Arguments:
- queries: bfloat16 [1024, 6144], P('ctx', 'exp'), may hold values from -8 to 8
- keys_values: bfloat16 [2, 1024, 1024], P(None, 'ctx', 'exp'), may hold values from -8 to 8
- residual: bfloat16 [1024, 6144], P(('ctx', 'exp')), may hold values from -12 to 12
- out_weight: bfloat16 [6144, 6144], P('exp', 'ctx'), may hold values from -0.078125 to 0.078125
- norm_gain: float32 [6144], replicated, may hold values from 0.5 to 2
- routes: int32 [1024, 4], P(('ctx', 'exp')), may hold values from 0 to 15, as said below
- route_weight: float32 [1024, 4], P(('ctx', 'exp')), may hold values from 0.1 to 1
- gate_weight: bfloat16 [16, 6144, 5376], P('exp', None, 'ctx'), may hold values from -0.078125 to 0.078125
- up_weight: bfloat16 [16, 6144, 5376], P('exp', None, 'ctx'), may hold values from -0.078125 to 0.078125
- down_weight: bfloat16 [16, 5376, 6144], P('exp', 'ctx'), may hold values from -0.078125 to 0.078125
Outputs:
- layer_out: bfloat16 [1024, 6144], P(('ctx', 'exp'))
Inputs may be any that keep to these rules, and one draw needn't show every extreme that they name: `routes`: each row names 4 different experts. Within each aligned block of 8 rows (the rows of one device) no expert is named by more than 4 rows, and one expert is named by exactly 4 rows in every block.
All inputs are finite; a program needn't handle non-finite values.
Results may differ from a plain program's by a relative error of at most 0.025.
Values may be sent and summed in bfloat16 or wider, within the bound.
A program may use at most 128 MiB of HBM per device.

v0:
```python
import math

import jax
import jax.numpy as jnp
from jax import lax
from jax.sharding import PartitionSpec as P

HD = 128


def from_partner(value, axis, bit):
    return lax.ppermute(value, axis, [(i, i ^ 1 << bit) for i in range(lax.axis_size(axis))])


def expert_partial(token_block, gate_weight, up_weight, down_weight):
    gate_part = jnp.einsum(
        "ind,df->inf", token_block, gate_weight[0], preferred_element_type=jnp.float32
    )
    up_part = jnp.einsum(
        "ind,df->inf", token_block, up_weight[0], preferred_element_type=jnp.float32
    )
    activated = (jax.nn.silu(gate_part) * up_part).astype(jnp.bfloat16)
    return jnp.einsum("inf,fd->ind", activated, down_weight[0], preferred_element_type=jnp.float32)


def on_device(
    queries,
    keys_values,
    residual,
    out_weight,
    norm_gain,
    routes,
    route_weight,
    gate_weight,
    up_weight,
    down_weight,
):
    context_devices = lax.axis_size("ctx")
    expert_devices = lax.axis_size("exp")
    block_rows = queries.shape[0]
    local_heads = queries.shape[1] // HD
    token_rows = residual.shape[0]
    features = residual.shape[1]
    partner = from_partner(keys_values, "exp", 0)
    is_lower = lax.axis_index("exp") % 2 == 0
    joined = jnp.where(
        is_lower,
        jnp.concatenate([keys_values, partner], axis=2),
        jnp.concatenate([partner, keys_values], axis=2),
    )
    query_heads = queries.reshape(block_rows, local_heads, HD)
    first_position = lax.axis_index("ctx") * block_rows
    query_position = first_position + jnp.arange(block_rows, dtype=jnp.int32)
    last_position = first_position + block_rows - 1
    initial = (
        jnp.full((local_heads, block_rows), -jnp.inf, jnp.float32),
        jnp.zeros((local_heads, block_rows), jnp.float32),
        jnp.zeros((local_heads, block_rows, HD), jnp.float32),
    )
    portion = lax.all_gather(joined, "ctx", axis=1, tiled=True)

    def update(current):
        running_max, denominator, weighted_sum = current
        scores = jnp.einsum(
            "qhd,kd->hqk", query_heads, portion[0], preferred_element_type=jnp.float32
        ) / math.sqrt(HD)
        key_position = jnp.arange(portion.shape[1], dtype=jnp.int32)
        allowed = key_position[None, None, :] <= query_position[None, :, None]
        masked = jnp.where(allowed, scores, -jnp.inf)
        new_max = jnp.max(masked, axis=2)
        safe_max = jnp.where(new_max == -jnp.inf, 0.0, new_max)
        weights_now = jnp.where(allowed, jnp.exp(masked - safe_max[:, :, None]), 0.0)
        rescale = jnp.exp(running_max - safe_max)
        denominator = rescale * denominator + jnp.sum(weights_now, axis=2)
        weighted_sum = rescale[:, :, None] * weighted_sum + jnp.einsum(
            "hqk,kd->hqd",
            weights_now,
            portion[1].astype(jnp.float32),
            precision=lax.Precision.HIGHEST,
        )
        return (new_max, denominator, weighted_sum)

    running_max, denominator, weighted_sum = lax.cond(
        jnp.int32(0) > last_position, lambda unchanged: unchanged, update, initial
    )
    attended = (
        (weighted_sum / denominator[:, :, None])
        .transpose(1, 0, 2)
        .reshape(block_rows, local_heads * HD)
        .astype(jnp.bfloat16)
    )
    partial_value = jnp.dot(
        attended,
        lax.all_gather(out_weight, "ctx", axis=1, tiled=True),
        preferred_element_type=jnp.float32,
    )
    projected = lax.psum_scatter(
        partial_value.astype(jnp.bfloat16), "exp", scatter_dimension=0, tiled=True
    ).astype(jnp.float32)
    hidden_state = residual.astype(jnp.float32) + projected
    row_mean = jnp.mean(hidden_state, axis=1, keepdims=True)
    centered = hidden_state - row_mean
    variance = jnp.mean(centered * centered, axis=1, keepdims=True)
    normed = (centered * lax.rsqrt(variance + 1e-05) * norm_gain).astype(jnp.bfloat16)
    fanout = routes.shape[1]
    capacity = 2 * token_rows * fanout // expert_devices
    flat_routes = routes.reshape(-1)
    selector = (
        flat_routes[:, None] == jnp.arange(expert_devices, dtype=jnp.int32)[None, :]
    ).astype(jnp.int32)
    earlier = jnp.cumsum(selector, axis=0) - selector
    slot_index = jnp.sum(earlier * selector, axis=1)
    target = flat_routes * capacity + slot_index
    source_rows = jnp.repeat(normed, fanout, axis=0)
    packed = (
        jnp.zeros((expert_devices * capacity, features), jnp.bfloat16).at[target].set(source_rows)
    )
    spread = jnp.broadcast_to(
        packed.reshape(1, expert_devices, capacity, features),
        (context_devices, expert_devices, capacity, features),
    )
    spread = spread.reshape(context_devices * expert_devices, capacity, features)
    partial_out = expert_partial(
        lax.all_to_all(spread, ("ctx", "exp"), split_axis=0, concat_axis=0, tiled=True),
        gate_weight,
        up_weight,
        down_weight,
    ).astype(jnp.bfloat16)
    returned = lax.all_to_all(partial_out, ("ctx", "exp"), split_axis=0, concat_axis=0, tiled=True)
    combined = jnp.sum(
        returned.reshape(context_devices, expert_devices * capacity, features).astype(jnp.float32),
        axis=0,
    )
    expert_out = combined[target]
    weighted = (expert_out * route_weight.reshape(-1)[:, None]).reshape(
        token_rows, fanout, features
    )
    return (hidden_state + jnp.sum(weighted, axis=1)).astype(jnp.bfloat16)


def solution(mesh):
    in_specs = (
        P("ctx", "exp"),
        P(None, "ctx", "exp"),
        P(("ctx", "exp"), None),
        P("exp", "ctx"),
        P(),
        P(("ctx", "exp"), None),
        P(("ctx", "exp"), None),
        P("exp", None, "ctx"),
        P("exp", None, "ctx"),
        P("exp", "ctx", None),
    )
    out_specs = P(("ctx", "exp"), None)
    return jax.shard_map(
        on_device, mesh=mesh, in_specs=in_specs, out_specs=out_specs, check_vma=False
    )
```

profile of v0, /device:TPU:0, one launch (start us, length us, event | category | flops | bytes accessed | tf_op | source)
XLA Modules:
  0.0 431.2 jit_solution(12090835512221466039)
XLA Ops:
  6.5 0.0 all-gather.2.cloned.1.call-start
  6.5 0.7 all-gather.2.cloned.1.call-update
  7.3 0.0 reduce-scatter.2.cloned.1.call-start
  7.3 0.9 copy.35
  8.2 0.1 collective-permute-start
  8.3 1.2 collective-permute-done
  9.5 0.1 maximum_select_fusion
  9.6 33.9 %all_gather.6 = bf16[2,1024,128]{2,1,0:T(8,128)(2,1)S(1)} all-gather(bf16[2,128,128]{2,1,0:T(8,128)(2,1)S(1)} %maximum_select_fusion), channel_id=1, replica_groups=mesh['ctx'=8,'exp'=16] {'ctx'}, dimensions={1}, use_global_device_ids=true | all-gather | bytes 589824 | tf_op jit(solution)/shard_map/all_gather | solution.py:60
  43.5 3.4 conditional.1
  43.5 0.1 iota_compare_fusion
  43.6 1.0 copy.37
  44.6 0.4 fusion.34
  45.0 0.3 fusion.1
  45.3 1.5 fusion.2
  46.8 0.1 copy.47
  46.9 71.5 %all-gather.2.cloned.1.call-done = bf16[384,6144]{1,0:T(8,128)(2,1)} async-done(((bf16[384,768]{1,0:T(8,128)(2,1)}), bf16[384,6144]{1,0:T(8,128)(2,1)}) %all-gather.2.cloned.1.call-update) | async-done | bytes 4718608 | tf_op jit(solution)/shard_map/all_gather | solution.py:94
  118.4 4.5 %convolution_convert_fusion.1 = bf16[128,6144]{1,0:T(8,128)(2,1)} fusion(bf16[128,384]{0,1:T(8,128)(2,1)S(1)} %bitcast.44, bf16[384,6144]{1,0:T(8,128)(2,1)} %all-gather.2.cloned.1.call-done), kind=kOutput, calls=%fused_computation.26 | convolution fusion | flops 604766208 | bytes 6389760 | tf_op jit(solution)/shard_map/dot_general | solution.py:92
  123.0 0.0 copy-start.3
  123.0 0.0 copy-start
  123.0 0.0 copy-start.2
  123.0 0.0 reduce-scatter.2.cloned.1.call-update
  123.0 0.7 copy-done.3
  123.6 0.1 copy.40
  123.7 0.1 eq.31
  123.8 0.1 fusion.32
  123.9 0.1 reduce_window_sum.11
  123.9 0.1 copy.39
  124.0 0.1 mul.70
  124.1 0.2 select_reduce_fusion
  124.3 67.7 %reduce-scatter.2.cloned.1.call-done = bf16[8,6144]{1,0:T(8,128)(2,1)} async-done(((bf16[128,6144]{1,0:T(8,128)(2,1)}), bf16[8,6144]{1,0:T(8,128)(2,1)}) %reduce-scatter.2.cloned.1.call-update) | async-done | bytes 98320 | tf_op jit(solution)/shard_map/reduce_scatter | solution.py:97
  192.0 0.0 copy-done
  192.0 1.1 fusion.31
  193.1 1.1 multiply_reduce_fusion.1
  194.2 0.0 copy-done.2
  194.2 1.0 multiply_convert_fusion
  195.2 0.1 broadcast_in_dim.55
  195.3 0.1 reshape.114
  195.4 1.4 scatter_custom_fusion
  196.8 0.3 broadcast_in_dim.56
  197.1 3.1 broadcast_in_dim.57
  200.2 0.0 slice-start
  200.2 82.5 %all_to_all.10 = bf16[128,4,6144]{2,1,0:T(4,128)(2,1)S(1)} all-to-all(bf16[128,4,6144]{2,1,0:T(4,128)(2,1)S(1)} %bitcast.43), channel_id=1, replica_groups=mesh['ctx'=8,'exp'=16] {'ctx','exp'}, dimensions={0} | all-to-all | bytes 12582912 | tf_op jit(solution)/shard_map/all_to_all | solution.py:124
  282.7 0.0 slice-start.1
  282.7 17.5 %fusion.15 = f32[128,4,672]{0,2,1:T(8,128)S(1)} fusion(bf16[1,6144,672]{1,2,0:T(8,128)(2,1)} %param.19, bf16[128,4,6144]{2,1,0:T(4,128)(2,1)S(1)} %all_to_all.10), kind=kOutput, calls=%fused_computation.24 | convolution fusion | flops 4227858432 | bytes 15925248 | tf_op jit(solution)/shard_map/ind,df->inf/dot_general | solution.py:16
  300.2 0.0 slice-done
  300.2 0.0 slice-done.1
  300.2 0.0 slice-start.3
  300.2 8.9 %fusion.24 = bf16[128,4,672]{0,2,1:T(8,128)(2,1)S(1)} fusion(bf16[1,6144,672]{1,2,0:T(8,128)(2,1)S(1)} %bitcast.47, bf16[128,4,6144]{2,1,0:T(4,128)(2,1)S(1)} %all_to_all.10, f32[128,4,672]{0,2,1:T(8,128)S(1)} %fusion.15), kind=kOutput, calls=%fused_computation.30 | convolution fusion | flops 4229922816 | bytes 16613376 | tf_op jit(solution)/shard_map/ind,df->inf/dot_general | solution.py:19
  309.1 0.0 slice-done.2
  309.1 0.0 slice-done.3
  309.1 5.8 %convolution_convert_fusion = bf16[128,4,6144]{2,0,1:T(8,128)(2,1)S(1)} fusion(bf16[128,4,672]{0,2,1:T(8,128)(2,1)S(1)} %fusion.24, bf16[1,672,6144]{2,1,0:T(8,128)(2,1)S(1)} %bitcast.49), kind=kOutput, calls=%fused_computation.20 | convolution fusion | flops 4231004160 | bytes 15237120 | tf_op jit(solution)/shard_map/inf,fd->ind/dot_general | solution.py:23
  314.9 7.5 %copy.43 = bf16[128,4,6144]{2,1,0:T(4,128)(2,1)} copy(bf16[128,4,6144]{2,0,1:T(8,128)(2,1)S(1)} %convolution_convert_fusion) | data formatting | bytes 12582912 | tf_op jit(solution)/shard_map/convert_element_type | solution.py:128
  322.4 7.3 %all-to-all-start.1 = ((bf16[128,4,6144]{2,1,0:T(4,128)(2,1)}), bf16[128,4,6144]{2,1,0:T(4,128)(2,1)}, u32[]{:S(2)}, u32[]{:S(2)}) async-start(bf16[128,4,6144]{2,1,0:T(4,128)(2,1)} %copy.43), calls=%async_computation.2 | async-start | bytes 12582912 | tf_op jit(solution)/shard_map/all_to_all | solution.py:129
  329.7 0.0 copy-done.4
  329.7 0.1 copy.44
  329.8 75.5 %all-to-all-done.1 = bf16[128,4,6144]{2,1,0:T(4,128)(2,1)} async-done(((bf16[128,4,6144]{2,1,0:T(4,128)(2,1)}), bf16[128,4,6144]{2,1,0:T(4,128)(2,1)}, u32[]{:S(2)}, u32[]{:S(2)}) %all-to-all-start.1) | async-done | bytes 6291488 | tf_op jit(solution)/shard_map/all_to_all | solution.py:129
  405.3 11.2 %reshape.101 = f32[8,64,6144]{2,1,0:T(8,128)} reshape(bf16[128,4,6144]{2,1,0:T(4,128)(2,1)} %all-to-all-done.1) | data formatting | bytes 18874368 | tf_op jit(solution)/shard_map/convert_element_type | solution.py:131
  416.5 5.5 %reduce_sum.60 = f32[64,6144]{1,0:T(8,128)S(1)} reduce(f32[8,64,6144]{2,1,0:T(8,128)} %reshape.101, f32[]{:T(128)} %constant.60.clone.1), dimensions={0}, to_apply=%region_10.11 | reduce | flops 2752512 | bytes 14155780 | tf_op jit(solution)/shard_map/reduce_sum | solution.py:130
  422.0 0.8 gather_fusion
  422.8 0.0 copy-start.1
  422.8 0.2 gather.6
  423.1 0.6 multiply_reduce_fusion
  423.6 0.1 copy-done.1
  423.7 0.7 add_convert_fusion
  (14 shorter events, 0.1 us)
Async XLA Ops:
  6.5 111.9 %all-gather.2.cloned.1.call-start = ((), (), s32[]{:S(2)}) async-start(), calls=%async_computation.3 | async-start | bytes 5308416 | tf_op jit(solution)/shard_map/all_gather | solution.py:94
  7.3 184.7 %reduce-scatter.2.cloned.1.call-start = ((), (), s32[]{:S(2)}) async-start(), calls=%async_computation.4 | async-start | bytes 1671168 | tf_op jit(solution)/shard_map/reduce_scatter | solution.py:97
  8.2 1.3 collective-permute-start
  123.0 0.7 copy-start.3
  123.0 69.0 %copy-start = (bf16[8,6144]{1,0:T(8,128)(2,1)S(1)}, bf16[8,6144]{1,0:T(8,128)(2,1)}, u32[]{:S(2)}) copy-start(bf16[8,6144]{1,0:T(8,128)(2,1)} %param.14) | copy-start | bytes 294916
  123.0 71.2 %copy-start.2 = (f32[6144]{0:T(1024)S(1)}, f32[6144]{0:T(1024)}, u32[]{:S(2)}) copy-start(f32[6144]{0:T(1024)} %param.16) | copy-start | bytes 73732
  200.2 100.0 %slice-start = ((s8[8257536]{0:T(1024)(128)(4,1)}), s8[4194304]{0:T(1024)(128)(4,1)S(1)}, s32[]{:S(2)}) async-start(s8[8257536]{0:T(1024)(128)(4,1)} %bitcast.46), calls=%async_computation.5 | async-start | bytes 8388608
  282.7 17.5 %slice-start.1 = ((s8[8257536]{0:T(1024)(128)(4,1)}), s8[4063232]{0:T(1024)(128)(4,1)S(1)}, s32[]{:S(2)}) async-start(s8[8257536]{0:T(1024)(128)(4,1)} %bitcast.46), calls=%async_computation.6 | async-start | bytes 8126464
  282.7 26.4 %slice-start.2 = ((s8[8257536]{0:T(1024)(128)(4,1)}), s8[4194304]{0:T(1024)(128)(4,1)S(1)}, s32[]{:S(2)}) async-start(s8[8257536]{0:T(1024)(128)(4,1)} %bitcast.48), calls=%async_computation.7 | async-start | bytes 8388608
  300.2 8.9 %slice-start.3 = ((s8[8257536]{0:T(1024)(128)(4,1)}), s8[4063232]{0:T(1024)(128)(4,1)S(1)}, s32[]{:S(2)}) async-start(s8[8257536]{0:T(1024)(128)(4,1)} %bitcast.48), calls=%async_computation.8 | async-start | bytes 8126464
  322.4 7.3 %copy-start.4 = (f32[8,4]{0,1:T(4,128)S(1)}, f32[8,4]{0,1:T(4,128)}, u32[]{:S(2)}) copy-start(f32[8,4]{0,1:T(4,128)} %param.18) | copy-start | bytes 388
  322.4 82.9 %all-to-all-start.1 = ((bf16[128,4,6144]{2,1,0:T(4,128)(2,1)}), bf16[128,4,6144]{2,1,0:T(4,128)(2,1)}, u32[]{:S(2)}, u32[]{:S(2)}) async-start(bf16[128,4,6144]{2,1,0:T(4,128)(2,1)} %copy.43), calls=%async_computation.2 | async-start | bytes 12582912 | tf_op jit(solution)/shard_map/all_to_all | solution.py:129
  422.8 0.9 copy-start.1
Sparse Core Ops, SparseCore 0:
  9.0 109.3 all-gather.1
  123.1 68.8 reduce-scatter.1
where the time goes:
time: 435 us; the launch traced here: 431 us
  waiting for transfers between devices  217 us (50%)
  blocking collectives  116 us (27%)
  matrix products  38.5 us (9%)
  local copies, waits for them, and re-layouts  28 us (6%)
  between operations  13.6 us (3%)
  other arithmetic  10.8 us (2%)
  starting transfers between devices  7.39 us (2%)
    all_to_all x1, blocking collectives, on_device(): lax.all_to_all(spread, ('ctx', 'exp'), split_axis=0, concat_axis=0, tiled...  82.5 us
    all_to_all x1, waiting for transfers between devices, on_device(): lax.all_to_all(partial_out, ('ctx', 'exp'), split_axis=0, concat_axis=0,...  75.5 us
    all_gather x1, waiting for transfers between devices, on_device(): lax.all_gather(out_weight, 'ctx', axis=1, tiled=True)  71.5 us
    reduce_scatter x1, waiting for transfers between devices, on_device(): lax.psum_scatter(partial_value.astype(jnp.bfloat16), 'exp', scatter_dimen...  67.7 us
    all_gather x1, blocking collectives, on_device(): portion = lax.all_gather(joined, 'ctx', axis=1, tiled=True)  33.9 us
    dot_general x1, matrix products, expert_partial(): jnp.einsum('ind,df->inf', token_block, gate_weight[0], preferred_element_...  17.5 us
    convert_element_type x1, local copies, waits for them, and re-layouts, on_device(): returned.reshape(context_devices, expert_devices * capacity, features)  11.2 us
    dot_general x1, matrix products, expert_partial(): jnp.einsum('ind,df->inf', token_block, up_weight[0], preferred_element_ty...  8.87 us
  transfers between devices with their start and end apart: 4, of which 4 were waited for; matrix products, arithmetic and copies ran while one was open for 1% of the time, Pallas kernels for 0%

commit v1 on v0

--- a/solution.py
+++ b/solution.py
@@ -3,6 +3,8 @@
 import jax
 import jax.numpy as jnp
 from jax import lax
+from jax.experimental import pallas as pl
+from jax.experimental.pallas import tpu as pltpu
 from jax.sharding import PartitionSpec as P
 
 HD = 128
@@ -12,15 +14,481 @@
     return lax.ppermute(value, axis, [(i, i ^ 1 << bit) for i in range(lax.axis_size(axis))])
 
 
-def expert_partial(token_block, gate_weight, up_weight, down_weight):
-    gate_part = jnp.einsum(
-        "ind,df->inf", token_block, gate_weight[0], preferred_element_type=jnp.float32
-    )
-    up_part = jnp.einsum(
-        "ind,df->inf", token_block, up_weight[0], preferred_element_type=jnp.float32
-    )
-    activated = (jax.nn.silu(gate_part) * up_part).astype(jnp.bfloat16)
-    return jnp.einsum("inf,fd->ind", activated, down_weight[0], preferred_element_type=jnp.float32)
+MESH = pl.DeviceIdType.MESH
+ORDERS = (("x", "y", "z"), ("y", "z", "x"), ("z", "x", "y"))
+OFFSETS = (0, -1, 1, 2)
+GROUPS_BACK = (2, 1, -1, 0)
+
+
+def place():
+    ctx = lax.axis_index("ctx")
+    exp = lax.axis_index("exp")
+    return {
+        "z": ctx // 2,
+        "x": ((exp // 2) % 2) * 2 + ctx % 2,
+        "y": exp // 4,
+        "k": exp % 2,
+    }
+
+
+def device_at(at):
+    return (at["z"] * 2 + at["x"] % 2, at["y"] * 4 + (at["x"] // 2) * 2 + at["k"])
+
+
+def moved(at, axis, by):
+    there = dict(at)
+    if axis == "k":
+        there["k"] = 1 - at["k"]
+    else:
+        there[axis] = (at[axis] + by + 4) % 4
+    return there
+
+
+def send(source, target, send_sem, recv_sem, device):
+    copy = pltpu.make_async_remote_copy(
+        src_ref=source,
+        dst_ref=target,
+        send_sem=send_sem,
+        recv_sem=recv_sem,
+        device_id=device,
+        device_id_type=MESH,
+    )
+    copy.start()
+    return copy
+
+
+def arrived(target, send_sem, recv_sem, device):
+    pltpu.make_async_remote_copy(
+        src_ref=target,
+        dst_ref=target,
+        send_sem=send_sem,
+        recv_sem=recv_sem,
+        device_id=device,
+        device_id_type=MESH,
+    ).wait_recv()
+
+
+def expert_kernel(
+    piece_ref,
+    hidden_ref,
+    pick_ref,
+    slot_ref,
+    share_ref,
+    gate_hbm,
+    up_hbm,
+    down_hbm,
+    out_ref,
+    gate,
+    up,
+    down,
+    rows,
+    relay3,
+    full3,
+    relay2,
+    full2,
+    relay1,
+    full1,
+    gate_sum,
+    up_sum,
+    mixed,
+    mixed_other,
+    load_sem,
+    s1,
+    r1,
+    s2,
+    r2,
+    s3,
+    r3,
+    sp,
+    rp,
+    sd,
+    rd,
+    bs3,
+    br3,
+    bs2,
+    br2,
+    bs1,
+    br1,
+):
+    at = place()
+    k = at["k"]
+    near = {(a, d): device_at(moved(at, a, d)) for a in "xyz" for d in (1, -1)}
+    partner = device_at(moved(at, "k", 1))
+
+    barrier = pltpu.get_barrier_semaphore()
+    for device in [*near.values(), partner]:
+        pl.semaphore_signal(barrier, inc=1, device_id=device, device_id_type=MESH)
+    pl.semaphore_wait(barrier, 7)
+
+    def ring(axis, by):
+        return (at[axis] + by + 4) % 4
+
+    def piece(q, d):
+        a1, a2, a3 = ORDERS[q]
+        return rows.at[k, q, at[a3], at[a2], ring(a1, d)]
+
+    def line(q, d):
+        a1, a2, a3 = ORDERS[q]
+        return rows.at[k, q, at[a3], ring(a2, d)]
+
+    def group(q, d, g):
+        a1, a2, a3 = ORDERS[q]
+        return rows.at[k, q, ring(a3, d), ring(a2, g)]
+
+    def group_other(q, d, g):
+        a1, a2, a3 = ORDERS[q]
+        return rows.at[1 - k, q, ring(a3, d), ring(a2, g)]
+
+    sent = []
+
+    def go(*args):
+        sent.append(send(*args))
+
+    for q in range(3):
+        a1 = ORDERS[q][0]
+        piece(q, 0)[...] = piece_ref[q]
+        for kind, d in ((0, 1), (1, -1)):
+            go(piece(q, 0), piece(q, 0), s1.at[q, kind], r1.at[q, kind], near[a1, d])
+
+    loads = [
+        pltpu.make_async_copy(gate_hbm.at[0], gate, load_sem.at[0]),
+        pltpu.make_async_copy(up_hbm.at[0], up, load_sem.at[1]),
+        pltpu.make_async_copy(down_hbm.at[0], down.at[0], load_sem.at[2]),
+    ]
+    for load in loads:
+        load.start()
+    go(down_hbm.at[0], down.at[1], sd.at[0], rd.at[0], partner)
+    gate_sum[...] = jnp.zeros_like(gate_sum)
+    up_sum[...] = jnp.zeros_like(up_sum)
+
+    def half(ref, index, width):
+        return ref.at[pl.ds(index * width, width)]
+
+    def relay(q, axis, whole, kind, width, ssem, rsem):
+        d = 1 if kind == 0 else -1
+        arrived(whole(-d), ssem[kind], rsem[kind], near[axis, -d])
+        part = half(whole(-d), kind, width)
+        go(part, part, ssem[2 + kind], rsem[2 + kind], near[axis, d])
+
+    def finish(q, axis, whole, width, ssem, rsem):
+        for kind in (0, 1):
+            d = 1 if kind == 0 else -1
+            arrived(half(whole(2), kind, width), ssem[2 + kind], rsem[2 + kind], near[axis, -d])
+
+    def sems(ref, *index):
+        return [ref.at[(*index, kind)] for kind in range(4)]
+
+    def to_ring(axis, whole, ssem, rsem):
+        for kind, d in ((0, 1), (1, -1)):
+            go(whole(0), whole(0), ssem[kind], rsem[kind], near[axis, d])
+
+    def forward(q, d, g):
+        go(group(q, d, g), group(q, d, g), sp.at[q, d % 4, g % 4], rp.at[q, d % 4, g % 4], partner)
+
+    def one_plane(q, g):
+        a3 = ORDERS[q][2]
+        return a3, (lambda d: group(q, d, g)), sems(s3, q, g % 4), sems(r3, q, g % 4)
+
+    for kind in (0, 1):
+        for q in range(3):
+            relay(q, ORDERS[q][0], lambda d: piece(q, d), kind, 1, sems(s1, q), sems(r1, q))
+    for q in range(3):
+        a1, a2, a3 = ORDERS[q]
+        finish(q, a1, lambda d: piece(q, d), 1, sems(s1, q), sems(r1, q))
+        to_ring(a2, lambda d: line(q, d), sems(s2, q), sems(r2, q))
+        to_ring(*one_plane(q, 0))
+        forward(q, 0, 0)
+    for kind in (0, 1):
+        g = -1 if kind == 0 else 1
+        for q in range(3):
+            a1, a2, a3 = ORDERS[q]
+            relay(q, a2, lambda d: line(q, d), kind, 2, sems(s2, q), sems(r2, q))
+            to_ring(*one_plane(q, g))
+            forward(q, 0, g)
+    for q in range(3):
+        a1, a2, a3 = ORDERS[q]
+        finish(q, a2, lambda d: line(q, d), 2, sems(s2, q), sems(r2, q))
+        to_ring(*one_plane(q, 2))
+        forward(q, 0, 2)
+
+    def index_of(q, i3, i2):
+        a1, a2, a3 = ORDERS[q]
+        where = {a3: i3, a2: i2, a1: slice(None)}
+        return where["z"], where["y"], where["x"]
+
+    def hidden_unit(q, d):
+        a1, a2, a3 = ORDERS[q]
+        for g in OFFSETS:
+            arrived(
+                group_other(q, d, g), sp.at[q, d % 4, g % 4], rp.at[q, d % 4, g % 4], partner
+            )
+        i3 = ring(a3, d)
+        number = lax.broadcasted_iota(jnp.int32, (256, 512), 0)
+        picker = jnp.where(number == pick_ref[q, i3], 1.0, 0.0).astype(jnp.bfloat16)
+        picked = []
+        for s in range(2):
+            both = jnp.concatenate(
+                [rows[c, q, i3, :, :, s].reshape(256, 512) for c in range(2)], axis=0
+            )
+            picked.append(
+                jnp.dot(picker, both, preferred_element_type=jnp.float32).astype(jnp.bfloat16)
+            )
+        for weight, total in ((gate, gate_sum), (up, up_sum)):
+            value = None
+            for h in range(2):
+                x = jnp.concatenate([p[h * 128 : h * 128 + 128] for p in picked], axis=1)
+                base = h * 3072 + q * 1024
+                term = jnp.dot(
+                    x, weight[base : base + 1024, :], preferred_element_type=jnp.float32
+                )
+                value = term if value is None else value + term
+            for i2 in range(4):
+                where = index_of(q, i3, i2)
+                total[where] += value[i2 * 32 : i2 * 32 + 32].reshape(4, 8, 672)
+
+    for t, g in enumerate(OFFSETS):
+        for q in range(3):
+            a3, whole, ssem, rsem = one_plane(q, g)
+            for kind in (0, 1):
+                relay(q, a3, whole, kind, 2, ssem, rsem)
+                forward(q, -1 if kind == 0 else 1, g)
+        if t == 0:
+            loads[0].wait()
+            loads[1].wait()
+        if t >= 1:
+            hidden_unit(t - 1, 0)
+    for t, g in enumerate(OFFSETS):
+        for q in range(3):
+            a3, whole, ssem, rsem = one_plane(q, g)
+            finish(q, a3, whole, 2, ssem, rsem)
+            forward(q, 2, g)
+        if t == 0:
+            for q in range(3):
+                hidden_unit(q, -1)
+        if t == 1:
+            for q in range(3):
+                hidden_unit(q, 1)
+    for q in range(3):
+        hidden_unit(q, 2)
+
+    number = lax.broadcasted_iota(jnp.int32, (256, 128), 1)
+    for z in range(4):
+        g = gate_sum[z].reshape(128, 672)
+        u = up_sum[z].reshape(128, 672)
+        activated = (g / (1.0 + jnp.exp(-g)) * u).astype(jnp.bfloat16)
+        spread = jnp.where(number == slot_ref[z], 1.0, 0.0).astype(jnp.bfloat16)
+        value = jnp.dot(spread, activated, preferred_element_type=jnp.float32) * share_ref[z]
+        mixed[0, z] = value[:128].astype(jnp.bfloat16)
+        mixed[1, z] = value[128:].astype(jnp.bfloat16)
+    go(mixed.at[1 - k], mixed_other, sd.at[1], rd.at[1], partner)
+    gate_sum[...] = mixed[k].astype(jnp.float32).reshape(4, 4, 4, 8, 672)
+    loads[2].wait()
+    arrived(down.at[1], sd.at[0], rd.at[0], partner)
+    arrived(mixed_other, sd.at[1], rd.at[1], partner)
+    up_sum[...] = mixed_other[...].astype(jnp.float32).reshape(4, 4, 4, 8, 672)
+    for copy in sent:
+        copy.wait_send()
+    sent.clear()
+
+    def down_unit(q, d):
+        i3 = ring(ORDERS[q][2], d)
+        a = [
+            jnp.concatenate(
+                [total[index_of(q, i3, i2)].reshape(32, 672) for i2 in range(4)], axis=0
+            ).astype(jnp.bfloat16)
+            for total in (gate_sum, up_sum)
+        ]
+        for s in range(2):
+            sides = []
+            for h in range(2):
+                base = h * 3072 + q * 1024 + s * 512
+                value = jnp.dot(
+                    a[0], down[0, :, base : base + 512], preferred_element_type=jnp.float32
+                ) + jnp.dot(
+                    a[1], down[1, :, base : base + 512], preferred_element_type=jnp.float32
+                )
+                sides.append(value.reshape(16, 8, 512))
+            joined = jnp.concatenate(sides, axis=1).astype(jnp.bfloat16)
+            rows[k, q, i3, :, :, s] = joined.reshape(4, 4, 16, 512)
+
+    def add_into(ref, *others):
+        value = ref[...].astype(jnp.float32)
+        for other in others:
+            value = value + other[...].astype(jnp.float32)
+        ref[...] = value.astype(jnp.bfloat16)
+
+    def first(axis, far, width, slots, ssem, rsem):
+        for kind, d in ((0, 1), (1, -1)):
+            go(half(far, kind, width), slots[kind], ssem[kind], rsem[kind], near[axis, d])
+
+    def second(axis, whole, width, slots, full, ssem, rsem):
+        for kind, d in ((0, 1), (1, -1)):
+            arrived(slots[kind], ssem[kind], rsem[kind], near[axis, -d])
+            add_into(half(whole(d), kind, width), slots[kind])
+            go(whole(d), full[kind], ssem[2 + kind], rsem[2 + kind], near[axis, d])
+
+    def third(axis, whole, full, ssem, rsem):
+        for kind, d in ((0, 1), (1, -1)):
+            arrived(full[kind], ssem[2 + kind], rsem[2 + kind], near[axis, -d])
+        add_into(whole(0), *full)
+
+    def pair(ref, *index):
+        return [ref.at[(*index, kind)] for kind in range(2)]
+
+    for q in range(3):
+        down_unit(q, 2)
+        for g in GROUPS_BACK:
+            first(
+                ORDERS[q][2],
+                group(q, 2, g),
+                2,
+                pair(relay3, q, g % 4),
+                sems(bs3, q, g % 4),
+                sems(br3, q, g % 4),
+            )
+    for q in range(3):
+        down_unit(q, 1)
+        down_unit(q, -1)
+        for g in GROUPS_BACK:
+            second(
+                ORDERS[q][2],
+                lambda d: group(q, d, g),
+                2,
+                pair(relay3, q, g % 4),
+                pair(full3, q, g % 4),
+                sems(bs3, q, g % 4),
+                sems(br3, q, g % 4),
+            )
+    for q in range(3):
+        down_unit(q, 0)
+
+    def args2(q):
+        return ORDERS[q][1], (lambda d: line(q, d)), sems(bs2, q), sems(br2, q)
+
+    for g in GROUPS_BACK:
+        for q in range(3):
+            third(
+                ORDERS[q][2],
+                lambda d: group(q, d, g),
+                pair(full3, q, g % 4),
+                sems(bs3, q, g % 4),
+                sems(br3, q, g % 4),
+            )
+            if g == 2:
+                first(
+                    ORDERS[q][1], line(q, 2), 2, pair(relay2, q), sems(bs2, q), sems(br2, q)
+                )
+        if g == -1:
+            for q in range(3):
+                axis, whole, ssem, rsem = args2(q)
+                second(axis, whole, 2, pair(relay2, q), pair(full2, q), ssem, rsem)
+    for q in range(3):
+        axis, whole, ssem, rsem = args2(q)
+        third(axis, whole, pair(full2, q), ssem, rsem)
+        first(ORDERS[q][0], piece(q, 2), 1, pair(relay1, q), sems(bs1, q), sems(br1, q))
+    for q in range(3):
+        second(
+            ORDERS[q][0],
+            lambda d: piece(q, d),
+            1,
+            pair(relay1, q),
+            pair(full1, q),
+            sems(bs1, q),
+            sems(br1, q),
+        )
+    for q in range(3):
+        ssem, rsem = sems(bs1, q), sems(br1, q)
+        for kind, d in ((0, 1), (1, -1)):
+            arrived(
+                full1.at[q, kind], ssem[2 + kind], rsem[2 + kind], near[ORDERS[q][0], -d]
+            )
+        for s in range(2):
+            value = piece(q, 0)[s].astype(jnp.float32)
+            for kind in range(2):
+                value = value + full1[q, kind, s].astype(jnp.float32)
+            for h in range(2):
+                base = h * 3072 + q * 1024 + s * 512
+                columns = slice(base, base + 512)
+                out_ref[:, columns] = (
+                    hidden_ref[:, columns] + value[h * 8 : h * 8 + 8]
+                ).astype(jnp.bfloat16)
+    for copy in sent:
+        copy.wait_send()
+
+
+def experts(normed, hidden_state, routes, route_weight, gate_weight, up_weight, down_weight):
+    piece = normed.reshape(8, 2, 3, 2, 512).transpose(2, 3, 1, 0, 4).reshape(3, 2, 16, 512)
+    numbers = jnp.arange(16, dtype=jnp.int32)
+    own = jnp.sum(
+        jnp.where(routes[:, :, None] == numbers, route_weight[:, :, None], 0.0), axis=1
+    )
+    shares = lax.all_gather(own, ("ctx", "exp"), axis=0, tiled=True)
+    mine = jnp.sum(jnp.where(numbers == lax.axis_index("exp"), shares, 0.0), axis=1)
+    mine = mine.reshape(4, 2, 4, 2, 2, 8).transpose(0, 2, 3, 1, 4, 5).reshape(4, 4, 4, 2, 8)
+    chosen = (mine > 0).astype(jnp.int32)
+    slot = jnp.cumsum(chosen, axis=-1) - chosen + 4 * jnp.arange(2, dtype=jnp.int32)[:, None]
+    letters = "zyx"
+    picks = []
+    for a1, a2, a3 in ORDERS:
+        turn = [letters.index(a) for a in (a3, a2, a1)]
+        t_slot = slot.transpose(*turn, 3, 4).reshape(4, 16, 2, 8)
+        t_chosen = chosen.transpose(*turn, 3, 4).reshape(4, 16, 2, 8)
+        chip = 8 * jnp.arange(16, dtype=jnp.int32)[:, None, None]
+        target = jnp.where(t_chosen > 0, t_slot + chip, -1024).transpose(0, 2, 1, 3)
+        sides = jnp.stack([target, target + 128], axis=3)
+        picks.append(sides.reshape(4, 1, 512))
+    pick = jnp.stack(picks)
+    chip = 8 * jnp.arange(16, dtype=jnp.int32)[:, None, None]
+    slots = jnp.where(chosen > 0, slot, -1024).reshape(4, 16, 2, 8) + chip
+    slots = slots.transpose(0, 2, 1, 3).reshape(4, 256, 1)
+    weights = mine.reshape(4, 16, 2, 8).transpose(0, 2, 1, 3).reshape(4, 256, 1)
+    vmem = pl.BlockSpec(memory_space=pltpu.VMEM)
+    hbm = pl.BlockSpec(memory_space=pl.ANY)
+    dma = pltpu.SemaphoreType.DMA
+    bf16 = jnp.bfloat16
+    return pl.pallas_call(
+        expert_kernel,
+        name="experts",
+        out_shape=jax.ShapeDtypeStruct((8, 6144), bf16),
+        in_specs=[vmem] * 5 + [hbm] * 3,
+        out_specs=vmem,
+        scratch_shapes=[
+            pltpu.VMEM((6144, 672), bf16),
+            pltpu.VMEM((6144, 672), bf16),
+            pltpu.VMEM((2, 672, 6144), bf16),
+            pltpu.VMEM((2, 3, 4, 4, 4, 2, 16, 512), bf16),
+            pltpu.VMEM((3, 4, 2, 2, 2, 16, 512), bf16),
+            pltpu.VMEM((3, 4, 2, 4, 2, 16, 512), bf16),
+            pltpu.VMEM((3, 2, 2, 2, 16, 512), bf16),
+            pltpu.VMEM((3, 2, 4, 2, 16, 512), bf16),
+            pltpu.VMEM((3, 2, 1, 16, 512), bf16),
+            pltpu.VMEM((3, 2, 2, 16, 512), bf16),
+            pltpu.VMEM((4, 4, 4, 8, 672), jnp.float32),
+            pltpu.VMEM((4, 4, 4, 8, 672), jnp.float32),
+            pltpu.VMEM((2, 4, 128, 672), bf16),
+            pltpu.VMEM((4, 128, 672), bf16),
+            dma((3,)),
+            dma((3, 4)),
+            dma((3, 4)),
+            dma((3, 4)),
+            dma((3, 4)),
+            dma((3, 4, 4)),
+            dma((3, 4, 4)),
+            dma((3, 4, 4)),
+            dma((3, 4, 4)),
+            dma((2,)),
+            dma((2,)),
+            dma((3, 4, 4)),
+            dma((3, 4, 4)),
+            dma((3, 4)),
+            dma((3, 4)),
+            dma((3, 4)),
+            dma((3, 4)),
+        ],
+        compiler_params=pltpu.CompilerParams(
+            collective_id=1, has_side_effects=True, vmem_limit_bytes=63 * 1024 * 1024
+        ),
+    )(piece, hidden_state, pick, slots, weights, gate_weight, up_weight, down_weight)
 
 
 def on_device(
@@ -102,40 +570,9 @@
     centered = hidden_state - row_mean
     variance = jnp.mean(centered * centered, axis=1, keepdims=True)
     normed = (centered * lax.rsqrt(variance + 1e-05) * norm_gain).astype(jnp.bfloat16)
-    fanout = routes.shape[1]
-    capacity = 2 * token_rows * fanout // expert_devices
-    flat_routes = routes.reshape(-1)
-    selector = (
-        flat_routes[:, None] == jnp.arange(expert_devices, dtype=jnp.int32)[None, :]
-    ).astype(jnp.int32)
-    earlier = jnp.cumsum(selector, axis=0) - selector
-    slot_index = jnp.sum(earlier * selector, axis=1)
-    target = flat_routes * capacity + slot_index
-    source_rows = jnp.repeat(normed, fanout, axis=0)
-    packed = (
-        jnp.zeros((expert_devices * capacity, features), jnp.bfloat16).at[target].set(source_rows)
-    )
-    spread = jnp.broadcast_to(
-        packed.reshape(1, expert_devices, capacity, features),
-        (context_devices, expert_devices, capacity, features),
-    )
-    spread = spread.reshape(context_devices * expert_devices, capacity, features)
-    partial_out = expert_partial(
-        lax.all_to_all(spread, ("ctx", "exp"), split_axis=0, concat_axis=0, tiled=True),
-        gate_weight,
-        up_weight,
-        down_weight,
-    ).astype(jnp.bfloat16)
-    returned = lax.all_to_all(partial_out, ("ctx", "exp"), split_axis=0, concat_axis=0, tiled=True)
-    combined = jnp.sum(
-        returned.reshape(context_devices, expert_devices * capacity, features).astype(jnp.float32),
-        axis=0,
-    )
-    expert_out = combined[target]
-    weighted = (expert_out * route_weight.reshape(-1)[:, None]).reshape(
-        token_rows, fanout, features
-    )
-    return (hidden_state + jnp.sum(weighted, axis=1)).astype(jnp.bfloat16)
+    return experts(
+        normed, hidden_state, routes, route_weight, gate_weight, up_weight, down_weight
+    )
 
 
 def solution(mesh):

time: 435 us -> 448 us (1.030)
  waiting for transfers between devices: 217 us -> 72.6 us
  blocking collectives: 116 us -> 212 us
  Pallas kernels: 0 us -> 93.1 us
  matrix products: 38.5 us -> 6.35 us
  starting transfers between devices: 7.39 us -> 0.13 us
  other arithmetic: 10.8 us -> 17.8 us
    all_gather x0 -> x1, blocking collectives: none -> 178 us  [experts(): shares = lax.all_gather(own, ('ctx', 'exp'), axis=0, tiled=True)]
    pallas_call x0 -> x1, Pallas kernels: none -> 93.1 us  [experts(): pl.pallas_call(expert_kernel, name='experts', out_shape=jax.ShapeDtypeStr...]
    all_to_all x1 -> x0, blocking collectives: 82.5 us -> none  [on_device(): lax.all_to_all(spread, ('ctx', 'exp'), split_axis=0, concat_axis=0, tiled...]
    all_to_all x1 -> x0, waiting for transfers between devices: 75.5 us -> none  [on_device(): lax.all_to_all(partial_out, ('ctx', 'exp'), split_axis=0, concat_axis=0,...]
    reduce_scatter x1, waiting for transfers between devices: 67.7 us -> 0.01 us  [on_device(): lax.psum_scatter(partial_value.astype(jnp.bfloat16), 'exp', scatter_dimen...]
    dot_general x3 -> x0, matrix products: 32.1 us -> none  [the longest x1 17.5 us: expert_partial(): jnp.einsum('ind,df->inf', token_block, gate_weight[0], preferred_element_...]
    unnamed x21 -> x8, local copies, waits for them, and re-layouts: 1.81 us -> 26.2 us
    convert_element_type x2 -> x1, local copies, waits for them, and re-layouts: 18.7 us -> 0.04 us  [experts(): chosen = (mine > 0).astype(jnp.int32)]
  transfers between devices with their start and end apart: 4 -> 3, of which waited for: 4 -> 2; matrix products, arithmetic and copies ran while one was open for 1% -> 10% of each run, Pallas kernels for 0% -> 0%
where the time goes in v1:
time: 448 us; the launch traced here: 447 us
  blocking collectives  212 us (47%)
  Pallas kernels  93.1 us (21%)
  waiting for transfers between devices  72.6 us (16%)
  local copies, waits for them, and re-layouts  31.2 us (7%)
  other arithmetic  17.8 us (4%)
  between operations  13.6 us (3%)
  matrix products  6.35 us (1%)
    all_gather x1, blocking collectives, experts(): shares = lax.all_gather(own, ('ctx', 'exp'), axis=0, tiled=True)  178 us
    pallas_call x1, Pallas kernels, experts(): pl.pallas_call(expert_kernel, name='experts', out_shape=jax.ShapeDtypeStr...  93.1 us
    all_gather x1, waiting for transfers between devices, on_device(): lax.all_gather(out_weight, 'ctx', axis=1, tiled=True)  71.5 us
    all_gather x1, blocking collectives, on_device(): portion = lax.all_gather(joined, 'ctx', axis=1, tiled=True)  33.9 us
    unnamed x8, local copies, waits for them, and re-layouts  26.2 us
    another operation x1, other arithmetic, experts(): jnp.cumsum(chosen, axis=-1) - chosen  11.3 us
  transfers between devices with their start and end apart: 3, of which 2 were waited for; matrix products, arithmetic and copies ran while one was open for 10% of the time, Pallas kernels for 0%

profile of v1, /device:TPU:0, one launch (start us, length us, event | category | flops | bytes accessed | tf_op | source)
XLA Modules:
  0.0 446.5 jit_solution(395556744706756376)
XLA Ops:
  6.5 0.0 all-gather.2.cloned.1.call-start
  6.5 0.7 all-gather.2.cloned.1.call-update
  7.3 0.0 reduce-scatter.2.cloned.1.call-start
  7.3 0.9 copy.110
  8.2 0.1 collective-permute-start
  8.3 0.8 select_reduce_fusion.1
  9.1 0.4 collective-permute-done
  9.5 0.1 maximum_select_fusion
  9.6 33.9 %all_gather.9 = bf16[2,1024,128]{2,1,0:T(8,128)(2,1)S(1)} all-gather(bf16[2,128,128]{2,1,0:T(8,128)(2,1)S(1)} %maximum_select_fusion), channel_id=1, replica_groups=mesh['ctx'=8,'exp'=16] {'ctx'}, dimensions={1}, use_global_device_ids=true | all-gather | bytes 589824 | tf_op jit(solution)/shard_map/all_gather | solution.py:528
  43.5 3.4 conditional.1
  43.5 1.0 copy.112
  44.5 0.1 iota_compare_fusion
  44.6 0.4 fusion.22
  45.0 0.3 fusion.1
  45.3 1.5 fusion.2
  46.8 0.1 copy.136
  46.9 71.5 %all-gather.2.cloned.1.call-done = bf16[384,6144]{1,0:T(8,128)(2,1)} async-done(((bf16[384,768]{1,0:T(8,128)(2,1)}), bf16[384,6144]{1,0:T(8,128)(2,1)}) %all-gather.2.cloned.1.call-update) | async-done | bytes 4718608 | tf_op jit(solution)/shard_map/all_gather | solution.py:562
  118.4 4.5 %convolution_convert_fusion = bf16[128,6144]{1,0:T(8,128)(2,1)} fusion(bf16[128,384]{0,1:T(8,128)(2,1)S(1)} %bitcast.93, bf16[384,6144]{1,0:T(8,128)(2,1)} %all-gather.2.cloned.1.call-done), kind=kOutput, calls=%fused_computation.18 | convolution fusion | flops 604766208 | bytes 6389760 | tf_op jit(solution)/shard_map/dot_general | solution.py:560
  122.9 0.0 reduce-scatter.2.cloned.1.call-update
  123.0 177.7 %all_gather.11 = f32[1024,16]{1,0:T(8,128)S(1)} all-gather(f32[8,16]{1,0:T(8,128)S(1)} %select_reduce_fusion.1), channel_id=1, replica_groups=mesh['ctx'=8,'exp'=16] {'ctx','exp'}, dimensions={0}, use_global_device_ids=true | all-gather | bytes 66048 | tf_op jit(solution)/shard_map/all_gather | solution.py:425
  300.7 0.2 select_reduce_fusion
  300.9 0.1 reshape.108
  301.2 11.3 %reduce_window_sum.13 = s32[4,4,4,2,8]{4,3,2,1,0:T(2,128)S(1)} reduce-window(s32[4,4,4,2,8]{4,3,2,1,0:T(2,128)S(1)} %bitcast.80, s32[]{:T(128)} %constant.33.clone.1), window={size=1x1x1x1x8 pad=0_0x0_0x0_0x0_0x7_0}, to_apply=%region_9.10 | reduce-window | flops 7168 | bytes 8196 | tf_op jit(solution)/shard_map/jit(cumsum)/reduce_window_sum | solution.py:429
  312.5 0.1 fusion.26
  312.7 0.1 fusion.27
  312.9 0.1 add_bitcast_fusion
  313.0 0.1 fusion.18
  313.1 0.1 fusion.15
  313.3 0.1 copy.120
  313.4 0.2 stack_reshape.12
  313.6 0.1 copy.126
  313.7 0.2 stack_reshape.14
  313.9 0.1 copy.123
  314.0 0.2 stack_reshape.13
  314.2 1.0 reshape.117.slot_ref
  315.2 1.0 reshape.118.share_ref
  316.2 11.9 %copy.132.gate_hbm = bf16[1,6144,672]{2,1,0:T(8,128)(2,1)} copy(bf16[1,6144,672]{1,2,0:T(8,128)(2,1)} %param.19) | data formatting | bytes 16515072 | tf_op args[7]
  328.1 0.0 copy-start
  328.1 0.0 copy-start.1
  328.1 11.8 %copy.133.up_hbm = bf16[1,6144,672]{2,1,0:T(8,128)(2,1)} copy(bf16[1,6144,672]{1,2,0:T(8,128)(2,1)} %param.20) | data formatting | bytes 16515072 | tf_op args[8]
  340.0 0.6 pad_add_fusion.3.pick_ref
  340.6 0.0 reduce-scatter.2.cloned.1.call-done
  340.6 0.0 copy-done
  340.6 1.7 convert_add_fusion
  342.3 1.1 multiply_reduce_fusion
  343.4 0.0 copy-done.1
  343.4 1.0 multiply_convert_fusion
  344.4 0.6 copy.143
  345.1 93.1 %experts.1 = bf16[8,6144]{1,0:T(8,128)(2,1)} custom-call(bf16[3,2,16,512]{3,2,1,0:T(8,128)(2,1)} %bitcast.94, f32[8,6144]{1,0:T(8,128)} %get-tuple-element.49.hidden_ref, s32[3,4,1,512]{3,2,1,0:T(1,128)} %pad_add_fusion.3.pick_ref, s32[4,256,1]{2,1,0:T(8,128)} %reshape.117.slot_ref, f32[4,256,1]{2,1,0:T(8,128)} %reshape.118.share_ref, ...), custom_call_target="tpu_custom_call" | custom-call | tf_op jit(solution)/shard_map/experts/pallas_call | solution.py:449
  438.1 1.5 copy.150
  (22 shorter events, 0.4 us)
Async XLA Ops:
  6.5 111.9 %all-gather.2.cloned.1.call-start = ((), (), s32[]{:S(2)}) async-start(), calls=%async_computation.1 | async-start | bytes 5308416 | tf_op jit(solution)/shard_map/all_gather | solution.py:562
  7.3 333.3 %reduce-scatter.2.cloned.1.call-start = ((), (), s32[]{:S(2)}) async-start(), calls=%async_computation.2 | async-start | bytes 1671168 | tf_op jit(solution)/shard_map/reduce_scatter | solution.py:565
  8.2 1.3 collective-permute-start
  328.1 12.4 %copy-start = (bf16[8,6144]{1,0:T(8,128)(2,1)S(1)}, bf16[8,6144]{1,0:T(8,128)(2,1)}, u32[]{:S(2)}) copy-start(bf16[8,6144]{1,0:T(8,128)(2,1)} %param.14) | copy-start | bytes 294916
  328.1 15.3 %copy-start.1 = (f32[6144]{0:T(1024)S(1)}, f32[6144]{0:T(1024)}, u32[]{:S(2)}) copy-start(f32[6144]{0:T(1024)} %param.16) | copy-start | bytes 73732
Sparse Core Ops, SparseCore 0:
  9.0 109.3 all-gather.1
  123.1 68.9 reduce-scatter.1

commit v2 on v0

v2 whole, which is shorter than its diff:
```python
import math
from types import SimpleNamespace

import jax
import jax.numpy as jnp
from jax import lax
from jax.experimental import pallas as pl
from jax.experimental.pallas import tpu as pltpu
from jax.sharding import PartitionSpec as P

HD = 128
MESH = pl.DeviceIdType.MESH
BF16 = jnp.bfloat16
F32 = jnp.float32
ORDERS = (("x", "y", "z"), ("y", "z", "x"), ("z", "x", "y"))
OFFSETS = (0, -1, 1, 2)
GROUPS_BACK = (2, 1, -1, 0)

SCRATCH = {
    "query": ((128, 384), BF16),
    "residual": ((8, 6144), BF16),
    "gain": ((1, 6144), F32),
    "routes": ((4, 8), jnp.int32),
    "share": ((4, 8), F32),
    "blocks": ((8, 2, 2, 64, 128), BF16),
    "attended": ((2, 64, 384), BF16),
    "partial_in": ((8, 2, 32, 768), BF16),
    "summed": ((8, 8, 768), F32),
    "summed_in": ((8, 8, 768), F32),
    "hidden": ((8, 6144), F32),
    "table": ((2, 8, 1, 128), F32),
    "table1": ((2, 8, 1, 128), F32),
    "table2": ((2, 8, 8, 1, 128), F32),
    "tables": ((2, 8, 8, 1, 128), F32),
    "targets": ((8, 1, 512), F32),
    "gate": ((672, 6144), BF16),
    "up": ((672, 6144), BF16),
    "down": ((2, 672, 6144), BF16),
    "rows": ((2, 3, 4, 4, 4, 2, 16, 512), BF16),
    "relay3": ((3, 2, 4, 2, 2, 16, 512), BF16),
    "full3": ((3, 2, 4, 2, 4, 16, 512), BF16),
    "full2": ((3, 2, 4, 4, 16, 512), BF16),
    "full1": ((3, 2, 4, 16, 512), BF16),
    "selected": ((512, 3072), BF16),
    "sums": ((512, 1536), F32),
    "mixed": ((2, 512, 672), BF16),
    "mixed_other": ((512, 672), BF16),
}
SEMAPHORES = {
    "load": (10,),
    "kv": (8,),
    "pair": (8,),
    "weight": (1,),
    "att": (8, 2),
    "sum": (8, 2),
    "back": (8,),
    "t1": (8,),
    "t2": (8,),
    "t3": (1,),
    "ag1": (3, 4),
    "ag2": (3, 4),
    "ag3": (3, 2, 4, 4),
    "fwd": (3, 2, 4, 4),
    "swap": (1,),
    "mix": (4,),
    "rs3": (3, 2, 4, 4),
    "rs2": (3, 2, 4),
    "rs1": (3, 2, 4),
}
INPUTS = (
    "query_hbm",
    "kv_hbm",
    "residual_hbm",
    "gain_hbm",
    "routes_hbm",
    "share_hbm",
    "weight_hbm",
    "gate_hbm",
    "up_hbm",
    "down_hbm",
)


def device_at(at):
    return (at["z"] * 2 + at["x"] % 2, at["y"] * 4 + (at["x"] // 2) * 2 + at["k"])


def moved(at, axis, by):
    there = dict(at)
    there[axis] = (at[axis] + by + 4) % 4
    return there


def column_of(h, s, q):
    return h * 3072 + s * 1536 + q * 512


class Links:
    def __init__(self, refs):
        self.refs = refs
        self.sent = []

    def copy(self, name, index, source, target, device):
        return pltpu.make_async_remote_copy(
            src_ref=source,
            dst_ref=target,
            send_sem=getattr(self.refs, name + "_s").at[index],
            recv_sem=getattr(self.refs, name + "_r").at[index],
            device_id=device,
            device_id_type=MESH,
        )

    def go(self, name, index, source, target, device):
        copy = self.copy(name, index, source, target, device)
        copy.start()
        self.sent.append(copy)

    def arrived(self, name, index, target, device):
        self.copy(name, index, target, target, device).wait_recv()

    def settle(self):
        for copy in self.sent:
            copy.wait_send()
        self.sent.clear()


def row_table(r, links, across, p):
    expert = lax.broadcasted_iota(jnp.int32, (16, 8), 0)
    chosen = jnp.zeros((16, 8), F32)
    share = jnp.zeros((16, 8), F32)
    for t in range(4):
        hit = jnp.where(r.routes[t : t + 1, :] == expert, 1.0, 0.0)
        chosen = chosen + hit
        share = share + hit * r.share[t : t + 1, :]
    upto = jnp.where(
        lax.broadcasted_iota(jnp.int32, (8, 8), 0) <= lax.broadcasted_iota(jnp.int32, (8, 8), 1),
        1.0,
        0.0,
    )
    code = chosen * jnp.dot(chosen, upto, preferred_element_type=F32)
    filled = jnp.concatenate([code, share, jnp.zeros((16, 112), F32)], axis=1)
    for i in range(16):
        r.table[i % 2, i // 2] = filled[i : i + 1]
    r.table1[:, p] = r.table[:, p]
    for i in range(1, 8):
        links.go("t1", i, r.table.at[:, (p + i) % 8], r.table1.at[:, p], across(i))


def layer_kernel(*refs):
    names = INPUTS + ("out",) + tuple(SCRATCH)
    for name in SEMAPHORES:
        names += (name + "_s", name + "_r")
    r = SimpleNamespace(**dict(zip(names, refs, strict=True)))
    links = Links(r)
    go, arrived = links.go, links.arrived

    c = lax.axis_index("ctx")
    e = lax.axis_index("exp")
    k = e % 2
    p = e // 2
    other = 2 * p + 1 - k
    partner = (c, other)
    at = {"z": c // 2, "x": (p % 2) * 2 + c % 2, "y": e // 4, "k": k}
    near = {(a, d): device_at(moved(at, a, d)) for a in "xyz" for d in (1, -1, 2, -2)}

    def along(j):
        return ((c + j) % 8, e)

    def along_other(j):
        return ((c + j) % 8, other)

    def across(i):
        return (c, 2 * ((p + i) % 8) + k)

    def load(i, source, target):
        copy = pltpu.make_async_copy(source, target, r.load_s.at[i])
        copy.start()
        return copy

    loads = [
        load(0, r.kv_hbm, r.blocks.at[c, k]),
        load(1, r.query_hbm, r.query),
        load(2, r.routes_hbm, r.routes),
        load(3, r.share_hbm, r.share),
        load(4, r.residual_hbm, r.residual),
        load(5, r.gain_hbm, r.gain),
    ]

    barrier = pltpu.get_barrier_semaphore()
    peers = [along(j) for j in range(1, 8)] + [along_other(j) for j in range(8)]
    peers += [across(i) for i in range(1, 8)] + [near["x", 1], near["x", -1]]
    for device in peers:
        pl.semaphore_signal(barrier, inc=1, device_id=device, device_id_type=MESH)
    pl.semaphore_wait(barrier, len(peers))

    loads[0].wait()
    own_block = r.blocks.at[c, k]
    go("pair", 0, own_block, own_block, partner)
    for j in range(1, 8):

        @pl.when(c + j < 8)
        def _(j=j):
            links.copy("kv", j, own_block, own_block, along(j)).start()

    def out_weight(side):
        return r.selected.at[pl.ds(0, 384), pl.ds(768 + side * 768, 768)]

    own_weight = load(6, r.weight_hbm, out_weight(k))
    go("weight", 0, r.weight_hbm, out_weight(k), partner)

    loads[2].wait()
    loads[3].wait()
    row_table(r, links, across, p)

    number = lax.broadcasted_iota(jnp.int32, (128, 128), 0)
    position = (number // 8 % 8) * 16 + (number // 64) * 8 + number % 8
    column = lax.broadcasted_iota(jnp.int32, (128, 128), 1)
    reorder = jnp.where(position == column, 1.0, 0.0).astype(BF16)
    loads[1].wait()
    turned = jnp.dot(reorder, r.query[...], preferred_element_type=F32)
    query = jnp.concatenate([turned[:, h * 128 : h * 128 + 128] for h in range(3)], axis=0)
    query = query.astype(BF16)

    for j in range(1, 8):

        @pl.when(c - j >= 0)
        def _(j=j):
            region = r.blocks.at[c - j, k]
            arrived("kv", j, region, along(8 - j))
            links.copy("pair", j, region, region, partner).start()

    big_loads = [
        load(7, r.gate_hbm.at[0], r.gate),
        load(8, r.up_hbm.at[0], r.up),
        load(9, r.down_hbm.at[0], r.down.at[0]),
    ]
    go("swap", 0, r.down_hbm.at[0], r.down.at[1], partner)

    for i in range(1, 8):
        arrived("t1", i, r.table1.at[:, (p - i + 8) % 8], across(8 - i))
    r.table2[:, c] = r.table1[...]
    for j in range(1, 8):
        go("t2", j, r.table1, r.table2.at[:, c], along(j))

    for j in range(8):
        columns = slice(j * 128, j * 128 + 128)

        @pl.when(c - j >= 0)
        def _(j=j, columns=columns):
            arrived("pair", j, r.blocks.at[c - j, 1 - k], partner)
            keys = jnp.concatenate([r.blocks[c - j, half, 0] for half in range(2)], axis=0)
            score = jnp.dot(query, keys, preferred_element_type=F32) / math.sqrt(HD)
            if j == 0:
                allowed = jnp.concatenate([column <= position] * 3, axis=0)
                score = jnp.where(allowed, score, -1e30)
            r.sums[0:384, columns] = score

        @pl.when(c - j < 0)
        def _(columns=columns):
            r.sums[0:384, columns] = jnp.full((384, 128), -1e30, F32)

    highest = jnp.max(r.sums[0:384, 0:1024], axis=1, keepdims=True)
    r.sums[0:384, 1024:1280] = jnp.zeros((384, 256), F32)
    for j in range(8):

        @pl.when(c - j >= 0)
        def _(j=j):
            now = jnp.exp(r.sums[0:384, j * 128 : j * 128 + 128] - highest)
            values = jnp.concatenate([r.blocks[c - j, half, 1] for half in range(2)], axis=0)
            r.sums[0:384, 1024:1152] += lax.dot_general(
                now.astype(BF16), values, (((1,), (1,)), ((), ())), preferred_element_type=F32
            )
            r.sums[0:384, 1152:1280] += now

    bottom = jnp.sum(r.sums[0:384, 1152:1280], axis=1, keepdims=True)
    result = (r.sums[0:384, 1024:1152] / bottom).astype(BF16)
    for h in range(3):
        for side in range(2):
            start = h * 128 + side * 64
            r.attended[side, :, h * 128 : h * 128 + 128] = result[start : start + 64]

    def gathered(b, side):
        return r.selected.at[pl.ds(b * 64, 64), pl.ds(pl.multiple_of(side * 384, 128), 384)]

    own_rows = pltpu.make_async_copy(r.attended.at[k], gathered(c, k), r.att_r.at[0, 0])
    own_rows.start()
    for j in range(8):
        if j > 0:
            go("att", (j, 0), r.attended.at[k], gathered(c, k), along(j))
        go("att", (j, 1), r.attended.at[1 - k], gathered(c, k), along_other(j))

    for j in range(1, 8):
        arrived("t2", j, r.table2.at[:, (c - j + 8) % 8], along(8 - j))
    r.tables[k] = r.table2[k]
    go("t3", 0, r.table2.at[1 - k], r.tables.at[k], partner)

    own_weight.wait()
    arrived("weight", 0, out_weight(1 - k), partner)

    def partial(i, part):
        return r.selected.at[pl.ds((i * 2 + part) * 32, 32), pl.ds(2304, 768)]

    for part in range(2):
        for b in range(part * 4, part * 4 + 4):
            j = (c - b + 8) % 8
            arrived("att", (j, 0), gathered(b, k), partner)
            arrived("att", (j, 1), gathered(b, 1 - k), partner)
        value = None
        for side in range(2):
            term = jnp.dot(
                r.selected[part * 256 : part * 256 + 256, side * 384 : side * 384 + 384],
                r.selected[0:384, 768 + side * 768 : 1536 + side * 768],
                preferred_element_type=F32,
            )
            value = term if value is None else value + term
        for i in range(8):
            partial(i, part)[...] = jnp.concatenate(
                [value[b * 64 + i * 8 : b * 64 + i * 8 + 8] for b in range(4)], axis=0
            ).astype(BF16)
        for i in range(1, 8):
            go("sum", (i, part), partial((p + i) % 8, part), r.partial_in.at[i, part], across(i))
    for part in range(2):
        value = partial(p, part)[...].astype(F32)
        for i in range(1, 8):
            arrived("sum", (i, part), r.partial_in.at[i, part], across(8 - i))
            value = value + r.partial_in[i, part].astype(F32)
        r.summed[part * 4 : part * 4 + 4] = value.reshape(4, 8, 768)
    r.summed_in[c] = r.summed[c]
    for j in range(1, 8):
        go("back", j, r.summed.at[(c + j) % 8], r.summed_in.at[c], along(j))
    for j in range(1, 8):
        arrived("back", j, r.summed_in.at[(c - j + 8) % 8], along(8 - j))
    for b in range(8):
        columns = slice(b * 768, b * 768 + 768)
        if b == 0:
            loads[4].wait()
            loads[5].wait()
        r.hidden[:, columns] = r.residual[:, columns].astype(F32) + r.summed_in[b]
    hidden = r.hidden[...]
    centered = hidden - jnp.mean(hidden, axis=1, keepdims=True)
    variance = jnp.mean(centered * centered, axis=1, keepdims=True)
    normed = centered * lax.rsqrt(variance + 1e-05) * r.gain[...]

    links.settle()

    def ring(axis, by):
        return (at[axis] + by + 4) % 4

    def piece(q, d):
        a1, a2, a3 = ORDERS[q]
        return r.rows.at[k, q, at[a3], at[a2], ring(a1, d)]

    def line(q, d):
        a1, a2, a3 = ORDERS[q]
        return r.rows.at[k, q, at[a3], ring(a2, d)]

    def group(q, s, d, g, side=None):
        a1, a2, a3 = ORDERS[q]
        side = k if side is None else side
        return r.rows.at[side, q, ring(a3, d), ring(a2, g), :, s]

    def half(ref, index):
        return ref.at[pl.ds(index * 2, 2)]

    for q in range(3):
        for s in range(2):
            low, high = column_of(0, s, q), column_of(1, s, q)
            piece(q, 0)[s] = jnp.concatenate(
                [normed[:, low : low + 512], normed[:, high : high + 512]], axis=0
            ).astype(BF16)
        for d in (1, -1, 2):
            go("ag1", (q, d % 4), piece(q, 0), piece(q, 0), near[ORDERS[q][0], d])

    arrived("t3", 0, r.tables.at[1 - k], partner)
    tables = r.tables[...].reshape(128, 128)
    table_high = tables.astype(BF16)
    table_low = (tables - table_high.astype(F32)).astype(BF16)

    def table_rows(turn, z):
        row = lax.broadcasted_iota(jnp.int32, (32, 128), 0)
        slow, fast = row // 4 % 4, row % 4
        x, y = (slow, fast) if turn else (fast, slow)
        source = row // 16 * 64 + z * 16 + x % 2 * 8 + y * 2 + x // 2
        wanted = source == lax.broadcasted_iota(jnp.int32, (32, 128), 1)
        chooser = jnp.where(wanted, 1.0, 0.0).astype(BF16)
        return jnp.dot(chooser, table_high, preferred_element_type=F32) + jnp.dot(
            chooser, table_low, preferred_element_type=F32
        )

    def pick_targets(turn, z):
        codes = table_rows(turn, z)[:, :8].astype(BF16)
        tile = lax.broadcasted_iota(jnp.int32, (8, 512), 1) % 8
        repeat = jnp.where(tile == lax.broadcasted_iota(jnp.int32, (8, 512), 0), 1.0, 0.0)
        spread = jnp.dot(codes, repeat.astype(BF16), preferred_element_type=F32)
        column = lax.broadcasted_iota(jnp.int32, (32, 512), 1)
        own = column // 16 == lax.broadcasted_iota(jnp.int32, (32, 512), 0)
        code = jnp.sum(jnp.where(own, spread, 0.0), axis=0, keepdims=True)
        column = lax.broadcasted_iota(jnp.int32, (1, 512), 1)
        chip = column // 16 % 16
        if turn:
            chip = chip % 4 * 4 + chip // 4
        base = column // 8 % 2 * 128 + chip * 8 + column // 256 * 4 - 1
        return jnp.where(code > 0, base.astype(F32) + code, -1.0)

    def slot_columns(z):
        found = table_rows(0, z)
        row = lax.broadcasted_iota(jnp.int32, (256, 32), 0)
        repeat = jnp.where(row // 8 == lax.broadcasted_iota(jnp.int32, (256, 32), 1), 1.0, 0.0)
        repeat = repeat.astype(BF16)
        high = found.astype(BF16)
        low = (found - high.astype(F32)).astype(BF16)
        spread = jnp.dot(repeat, high, preferred_element_type=F32) + jnp.dot(
            repeat, low, preferred_element_type=F32
        )
        lane = lax.broadcasted_iota(jnp.int32, (256, 128), 1)
        row = lax.broadcasted_iota(jnp.int32, (256, 128), 0)
        code = jnp.sum(jnp.where(lane == row % 8, spread, 0.0), axis=1, keepdims=True)
        share = jnp.sum(jnp.where(lane == row % 8 + 8, spread, 0.0), axis=1, keepdims=True)
        row = lax.broadcasted_iota(jnp.int32, (256, 1), 0)
        base = row // 8 % 16 * 8 + row // 128 * 4 - 1
        return jnp.where(code > 0, base.astype(F32) + code, -1.0), share

    def forward(q, s, d, g):
        region = group(q, s, d, g)
        go("fwd", (q, s, d % 4, g % 4), region, region, partner)

    def ring_send(q, s, g):
        for kind, d in ((0, 1), (1, -1)):
            region = group(q, s, 0, g)
            go("ag3", (q, s, g % 4, kind), region, region, near[ORDERS[q][2], d])

    def ring_relay(q, s, g):
        for kind, d in ((0, 1), (1, -1)):
            whole = group(q, s, -d, g)
            arrived("ag3", (q, s, g % 4, kind), whole, near[ORDERS[q][2], -d])
            part = half(whole, kind)
            go("ag3", (q, s, g % 4, 2 + kind), part, part, near[ORDERS[q][2], d])
            forward(q, s, -d, g)

    def ring_finish(q, s, g):
        for kind, d in ((0, 1), (1, -1)):
            part = half(group(q, s, 2, g), kind)
            arrived("ag3", (q, s, g % 4, 2 + kind), part, near[ORDERS[q][2], -d])
        forward(q, s, 2, g)

    for q in range(3):
        for d in (1, -1, 2):
            arrived("ag1", (q, d % 4), piece(q, -d), near[ORDERS[q][0], -d])
        for d in (1, -1, 2):
            go("ag2", (q, d % 4), line(q, 0), line(q, 0), near[ORDERS[q][1], d])
        ring_send(q, 0, 0)
        for s in range(2):
            forward(q, s, 0, 0)
    for z in range(4):
        for turn in range(2):
            r.targets[turn * 4 + z] = pick_targets(turn, z)
    for g in (-1, 1, 2):
        for q in range(3):
            arrived("ag2", (q, -g % 4), line(q, g), near[ORDERS[q][1], g])
            ring_send(q, 0, g)
            for s in range(2):
                forward(q, s, 0, g)
    for g in OFFSETS:
        for q in range(3):
            ring_relay(q, 0, g)
            ring_send(q, 1, g)
    for g in OFFSETS:
        for q in range(3):
            ring_finish(q, 0, g)

    def select(s):
        for q in range(3):
            for d in OFFSETS:
                for g in OFFSETS:
                    arrived(
                        "fwd", (q, s, d % 4, g % 4), group(q, s, d, g, 1 - k), partner
                    )
        slots = lax.broadcasted_iota(jnp.int32, (256, 512), 0).astype(F32)
        for z in range(4):
            for q in range(3):
                picker = jnp.where(slots == r.targets[(4 if q == 1 else 0) + z], 1.0, 0.0)
                sides = []
                for side in range(2):
                    found = (
                        r.rows[side, q, z, :, :, s],
                        r.rows[side, q, :, z, :, s],
                        r.rows[side, q, :, :, z, s],
                    )[q]
                    sides.append(found.reshape(256, 512))
                value = jnp.dot(
                    picker.astype(BF16),
                    jnp.concatenate(sides, axis=0),
                    preferred_element_type=F32,
                ).astype(BF16)
                for h in range(2):
                    start = h * 1536 + q * 512
                    r.selected[z * 128 : z * 128 + 128, start : start + 512] = value[
                        h * 128 : h * 128 + 128
                    ]

    def product(weight, s):
        value = None
        for h in range(2):
            start = column_of(h, s, 0)
            term = lax.dot_general(
                r.selected[:, h * 1536 : h * 1536 + 1536],
                weight[:, start : start + 1536],
                (((1,), (1,)), ((), ())),
                preferred_element_type=F32,
            )
            value = term if value is None else value + term
        return value

    select(0)
    for q in range(3):
        ring_relay(q, 1, 0)
    big_loads[0].wait()
    r.sums[:, 0:672] = product(r.gate, 0)
    for g in (-1, 1):
        for q in range(3):
            ring_relay(q, 1, g)
    big_loads[1].wait()
    r.sums[:, 768:1440] = product(r.up, 0)
    for q in range(3):
        ring_relay(q, 1, 2)
    for g in OFFSETS:
        for q in range(3):
            ring_finish(q, 1, g)
    select(1)
    r.sums[:, 0:672] += product(r.gate, 1)
    r.sums[:, 768:1440] += product(r.up, 1)

    number = lax.broadcasted_iota(jnp.int32, (256, 128), 1).astype(F32)
    for z in range(4):
        block = slice(z * 128, z * 128 + 128)
        g = r.sums[block, 0:672]
        u = r.sums[block, 768:1440]
        activated = (g / (1.0 + jnp.exp(-g)) * u).astype(BF16)
        place_of, share = slot_columns(z)
        spread = jnp.where(number == place_of, 1.0, 0.0).astype(BF16)
        value = jnp.dot(spread, activated, preferred_element_type=F32) * share
        r.mixed[0, block] = value[:128].astype(BF16)
        r.mixed[1, block] = value[128:].astype(BF16)
        go(
            "mix",
            z,
            r.mixed.at[1 - k, pl.ds(z * 128, 128)],
            r.mixed_other.at[pl.ds(z * 128, 128)],
            partner,
        )
    big_loads[2].wait()
    arrived("swap", 0, r.down.at[1], partner)
    for z in range(4):
        arrived("mix", z, r.mixed_other.at[pl.ds(z * 128, 128)], partner)
    links.settle()

    def down_unit(q, s):
        sides = []
        for h in range(2):
            start = column_of(h, s, q)
            value = jnp.dot(
                r.mixed[k], r.down[0, :, start : start + 512], preferred_element_type=F32
            ) + jnp.dot(
                r.mixed_other[...], r.down[1, :, start : start + 512], preferred_element_type=F32
            )
            sides.append(value.reshape(64, 8, 512))
        joined = jnp.concatenate(sides, axis=1).astype(BF16).reshape(4, 4, 4, 16, 512)
        if q == 0:
            r.rows[k, 0, :, :, :, s] = joined
        elif q == 1:
            for x in range(4):
                r.rows[k, 1, x, :, :, s] = joined[:, :, x]
        else:
            for y in range(4):
                for x in range(4):
                    r.rows[k, 2, y, x, :, s] = joined[:, y, x]

    def add_into(ref, *others):
        value = ref[...].astype(F32)
        for other_ref in others:
            value = value + other_ref[...].astype(F32)
        ref[...] = value.astype(BF16)

    def back_first(q, s):
        for g in GROUPS_BACK:
            for kind, d in ((0, 1), (1, -1)):
                go(
                    "rs3",
                    (q, s, g % 4, kind),
                    half(group(q, s, 2, g), kind),
                    r.relay3.at[q, s, g % 4, kind],
                    near[ORDERS[q][2], d],
                )

    def back_second(q, s):
        for g in GROUPS_BACK:
            for kind, d in ((0, 1), (1, -1)):
                slot = r.relay3.at[q, s, g % 4, kind]
                arrived("rs3", (q, s, g % 4, kind), slot, near[ORDERS[q][2], -d])
                whole = group(q, s, d, g)
                add_into(half(whole, kind), slot)
                go(
                    "rs3",
                    (q, s, g % 4, 2 + kind),
                    whole,
                    r.full3.at[q, s, g % 4, kind],
                    near[ORDERS[q][2], d],
                )

    def back_third(q, s, g):
        slots = [r.full3.at[q, s, g % 4, kind] for kind in range(2)]
        for kind, d in ((0, 1), (1, -1)):
            arrived("rs3", (q, s, g % 4, 2 + kind), slots[kind], near[ORDERS[q][2], -d])
        whole = group(q, s, 0, g)
        add_into(whole, *slots)
        if g != 0:
            go("rs2", (q, s, g % 4), whole, r.full2.at[q, s, g % 4], near[ORDERS[q][1], g])

    def back_line(q, s):
        slots = [r.full2.at[q, s, g % 4] for g in (1, -1, 2)]
        for g, slot in zip((1, -1, 2), slots, strict=True):
            arrived("rs2", (q, s, g % 4), slot, near[ORDERS[q][1], -g])
        add_into(group(q, s, 0, 0), *slots)
        for d in (1, -1, 2):
            go(
                "rs1",
                (q, s, d % 4),
                piece(q, d).at[s],
                r.full1.at[q, s, d % 4],
                near[ORDERS[q][0], d],
            )

    def back_end(q, s):
        value = piece(q, 0)[s].astype(F32)
        for d in (1, -1, 2):
            slot = r.full1.at[q, s, d % 4]
            arrived("rs1", (q, s, d % 4), slot, near[ORDERS[q][0], -d])
            value = value + slot[...].astype(F32)
        for h in range(2):
            start = column_of(h, s, q)
            columns = slice(start, start + 512)
            r.out[:, columns] = (r.hidden[:, columns] + value[h * 8 : h * 8 + 8]).astype(BF16)

    for q in range(3):
        down_unit(q, 0)
        back_first(q, 0)
    for q in range(3):
        down_unit(q, 1)
        back_first(q, 1)
        back_second(q, 0)
    for q in range(3):
        back_second(q, 1)
    for s in range(2):
        for g in GROUPS_BACK:
            for q in range(3):
                back_third(q, s, g)
    for s in range(2):
        for q in range(3):
            back_line(q, s)
    for s in range(2):
        for q in range(3):
            back_end(q, s)

    links.settle()
    for j in range(1, 8):

        @pl.when(c + j < 8)
        def _(j=j):
            links.copy("kv", j, own_block, own_block, along(j)).wait_send()

        @pl.when(c - j >= 0)
        def _(j=j):
            region = r.blocks.at[c - j, k]
            links.copy("pair", j, region, region, partner).wait_send()


def on_device(
    queries,
    keys_values,
    residual,
    out_weight,
    norm_gain,
    routes,
    route_weight,
    gate_weight,
    up_weight,
    down_weight,
):
    scratch = [pltpu.VMEM(shape, kind) for shape, kind in SCRATCH.values()]
    for shape in SEMAPHORES.values():
        scratch += [pltpu.SemaphoreType.DMA(shape)] * 2
    return pl.pallas_call(
        layer_kernel,
        name="layer",
        out_shape=jax.ShapeDtypeStruct(residual.shape, BF16),
        in_specs=[pl.BlockSpec(memory_space=pl.ANY)] * len(INPUTS),
        out_specs=pl.BlockSpec(memory_space=pltpu.VMEM),
        scratch_shapes=scratch,
        compiler_params=pltpu.CompilerParams(
            collective_id=1, has_side_effects=True, vmem_limit_bytes=64 * 1024 * 1024 - 65536
        ),
    )(
        queries,
        keys_values.swapaxes(1, 2),
        residual,
        norm_gain.reshape(1, -1),
        routes.T,
        route_weight.T,
        out_weight,
        gate_weight.swapaxes(1, 2),
        up_weight.swapaxes(1, 2),
        down_weight,
    )


def solution(mesh):
    in_specs = (
        P("ctx", "exp"),
        P(None, "ctx", "exp"),
        P(("ctx", "exp"), None),
        P("exp", "ctx"),
        P(),
        P(("ctx", "exp"), None),
        P(("ctx", "exp"), None),
        P("exp", None, "ctx"),
        P("exp", None, "ctx"),
        P("exp", "ctx", None),
    )
    out_specs = P(("ctx", "exp"), None)
    return jax.shard_map(
        on_device, mesh=mesh, in_specs=in_specs, out_specs=out_specs, check_vma=False
    )
```

time: 435 us -> 140 us (0.32)
  waiting for transfers between devices: 217 us -> 0 us
  Pallas kernels: 0 us -> 138 us
  blocking collectives: 116 us -> 0 us
  matrix products: 38.5 us -> 0 us
  local copies, waits for them, and re-layouts: 28 us -> 1.54 us
  between operations: 13.6 us -> 0.01 us
  other arithmetic: 10.8 us -> 0 us
  starting transfers between devices: 7.39 us -> 0 us
    pallas_call x0 -> x1, Pallas kernels: none -> 138 us  [on_device(): pl.pallas_call(layer_kernel, name='layer', out_shape=jax.ShapeDtypeStruct...]
    all_to_all x1 -> x0, blocking collectives: 82.5 us -> none  [on_device(): lax.all_to_all(spread, ('ctx', 'exp'), split_axis=0, concat_axis=0, tiled...]
    all_to_all x1 -> x0, waiting for transfers between devices: 75.5 us -> none  [on_device(): lax.all_to_all(partial_out, ('ctx', 'exp'), split_axis=0, concat_axis=0,...]
    all_gather x1 -> x0, waiting for transfers between devices: 71.5 us -> none  [on_device(): lax.all_gather(out_weight, 'ctx', axis=1, tiled=True)]
    reduce_scatter x1 -> x0, waiting for transfers between devices: 67.7 us -> none  [on_device(): lax.psum_scatter(partial_value.astype(jnp.bfloat16), 'exp', scatter_dimen...]
    dot_general x6 -> x0, matrix products: 38.5 us -> none  [the longest x1 17.5 us: expert_partial(): jnp.einsum('ind,df->inf', token_block, gate_weight[0], preferred_element_...]
    all_gather x1 -> x0, blocking collectives: 33.9 us -> none  [on_device(): portion = lax.all_gather(joined, 'ctx', axis=1, tiled=True)]
    convert_element_type x2 -> x0, local copies, waits for them, and re-layouts: 18.7 us -> none  [the longest x1 11.2 us: on_device(): returned.reshape(context_devices, expert_devices * capacity, features)]
  transfers between devices with their start and end apart: 4 -> 0, of which waited for: 4 -> 0; matrix products, arithmetic and copies ran while one was open for 1% -> 0% of each run, Pallas kernels for 0% -> 0%
where the time goes in v2:
time: 140 us
  Pallas kernels  138 us (99%)
  local copies, waits for them, and re-layouts  1.54 us (1%)
    pallas_call x1, Pallas kernels, on_device(): pl.pallas_call(layer_kernel, name='layer', out_shape=jax.ShapeDtypeStruct...  138 us

profile of v2, /device:TPU:0, one launch (start us, length us, event | category | flops | bytes accessed | tf_op | source)
XLA Modules:
  0.0 140.0 jit_solution(5167501579591513174)
XLA Ops:
  0.0 138.4 %layer.1 = bf16[8,6144]{1,0:T(8,128)(2,1)} custom-call(bf16[128,384]{1,0:T(8,128)(2,1)} %refs_0_.1, bf16[2,64,128]{2,1,0:T(8,128)(2,1)} %bitcast.8, bf16[8,6144]{1,0:T(8,128)(2,1)} %refs_2_.1, f32[1,6144]{1,0:T(1,128)} %bitcast.9, s32[4,8]{1,0:T(4,128)} %bitcast.10, f32[4,8]{1,0:T(4,128)} %bitcast.11, bf16[384,768]{1,0:T(8,128)(2,1)} %refs_6_.1, ...), custom_call_target="tpu_custom_call" | custom-call | tf_op jit(solution)/shard_map/layer/pallas_call | solution.py:692
  138.4 1.5 %copy.12 = bf16[8,6144]{1,0:T(8,128)(2,1)} copy(bf16[8,6144]{1,0:T(8,128)(2,1)} %layer.1) | data formatting | bytes 196608

commit v3 on v2

--- a/solution.py
+++ b/solution.py
@@ -24,7 +24,7 @@
     "share": ((4, 8), F32),
     "blocks": ((8, 2, 2, 64, 128), BF16),
     "attended": ((2, 64, 384), BF16),
-    "partial_in": ((8, 2, 32, 768), BF16),
+    "partial_in": ((2, 8, 32, 768), BF16),
     "summed": ((8, 8, 768), F32),
     "summed_in": ((8, 8, 768), F32),
     "hidden": ((8, 6144), F32),
@@ -46,26 +46,48 @@
     "mixed": ((2, 512, 672), BF16),
     "mixed_other": ((512, 672), BF16),
 }
-SEMAPHORES = {
+SENDS = {
     "load": (10,),
     "kv": (8,),
     "pair": (8,),
     "weight": (1,),
-    "att": (8, 2),
-    "sum": (8, 2),
-    "back": (8,),
-    "t1": (8,),
-    "t2": (8,),
+    "att": (1,),
+    "sum": (1,),
+    "back": (1,),
+    "t1": (1,),
+    "t2": (1,),
     "t3": (1,),
-    "ag1": (3, 4),
+    "ag1": (1,),
+    "ag2": (1,),
+    "ag3": (1,),
+    "fwd": (1,),
+    "swap": (1,),
+    "mix": (1,),
+    "rs3": (1,),
+    "rs2": (1,),
+    "rs1": (1,),
+}
+RECEIVES = {
+    "kv": (8,),
+    "pair": (8,),
+    "weight": (1,),
+    "att": (2,),
+    "sum": (2,),
+    "back": (1,),
+    "t1": (1,),
+    "t2": (1,),
+    "t3": (1,),
+    "ag1": (3,),
     "ag2": (3, 4),
-    "ag3": (3, 2, 4, 4),
-    "fwd": (3, 2, 4, 4),
+    "ag3": (3, 2, 4, 2),
+    "ag3end": (3, 2, 2),
+    "fwd": (3, 2),
     "swap": (1,),
-    "mix": (4,),
-    "rs3": (3, 2, 4, 4),
-    "rs2": (3, 2, 4),
-    "rs1": (3, 2, 4),
+    "mix": (1,),
+    "rs3": (3, 2, 4, 2),
+    "rs3end": (3, 2, 4),
+    "rs2": (3, 2),
+    "rs1": (3, 2),
 }
 INPUTS = (
     "query_hbm",
@@ -98,30 +120,25 @@
 class Links:
     def __init__(self, refs):
         self.refs = refs
-        self.sent = []
-
-    def copy(self, name, index, source, target, device):
+
+    def copy(self, send, receive, source, target, device):
         return pltpu.make_async_remote_copy(
             src_ref=source,
             dst_ref=target,
-            send_sem=getattr(self.refs, name + "_s").at[index],
-            recv_sem=getattr(self.refs, name + "_r").at[index],
+            send_sem=getattr(self.refs, send[0] + "_s").at[send[1]],
+            recv_sem=getattr(self.refs, receive[0] + "_r").at[receive[1]],
             device_id=device,
             device_id_type=MESH,
         )
 
-    def go(self, name, index, source, target, device):
-        copy = self.copy(name, index, source, target, device)
-        copy.start()
-        self.sent.append(copy)
+    def go(self, send, receive, source, target, device):
+        self.copy(send, receive, source, target, device).start()
 
     def arrived(self, name, index, target, device):
-        self.copy(name, index, target, target, device).wait_recv()
-
-    def settle(self):
-        for copy in self.sent:
-            copy.wait_send()
-        self.sent.clear()
+        self.copy((next(iter(SENDS)), 0), (name, index), target, target, device).wait_recv()
+
+    def left(self, name, index, source, device):
+        self.copy((name, index), (next(iter(RECEIVES)), 0), source, source, device).wait_send()
 
 
 def row_table(r, links, across, p):
@@ -143,16 +160,17 @@
         r.table[i % 2, i // 2] = filled[i : i + 1]
     r.table1[:, p] = r.table[:, p]
     for i in range(1, 8):
-        links.go("t1", i, r.table.at[:, (p + i) % 8], r.table1.at[:, p], across(i))
+        there = r.table.at[:, (p + i) % 8]
+        links.go(("t1", 0), ("t1", 0), there, r.table1.at[:, p], across(i))
 
 
 def layer_kernel(*refs):
     names = INPUTS + ("out",) + tuple(SCRATCH)
-    for name in SEMAPHORES:
-        names += (name + "_s", name + "_r")
+    names += tuple(name + "_s" for name in SENDS)
+    names += tuple(name + "_r" for name in RECEIVES)
     r = SimpleNamespace(**dict(zip(names, refs, strict=True)))
     links = Links(r)
-    go, arrived = links.go, links.arrived
+    go, arrived, left = links.go, links.arrived, links.left
 
     c = lax.axis_index("ctx")
     e = lax.axis_index("exp")
@@ -195,18 +213,18 @@
 
     loads[0].wait()
     own_block = r.blocks.at[c, k]
-    go("pair", 0, own_block, own_block, partner)
+    go(("pair", 0), ("pair", 0), own_block, own_block, partner)
     for j in range(1, 8):
 
         @pl.when(c + j < 8)
         def _(j=j):
-            links.copy("kv", j, own_block, own_block, along(j)).start()
+            go(("kv", j), ("kv", j), own_block, own_block, along(j))
 
     def out_weight(side):
         return r.selected.at[pl.ds(0, 384), pl.ds(768 + side * 768, 768)]
 
     own_weight = load(6, r.weight_hbm, out_weight(k))
-    go("weight", 0, r.weight_hbm, out_weight(k), partner)
+    go(("weight", 0), ("weight", 0), r.weight_hbm, out_weight(k), partner)
 
     loads[2].wait()
     loads[3].wait()
@@ -227,20 +245,19 @@
         def _(j=j):
             region = r.blocks.at[c - j, k]
             arrived("kv", j, region, along(8 - j))
-            links.copy("pair", j, region, region, partner).start()
+            go(("pair", j), ("pair", j), region, region, partner)
 
     big_loads = [
         load(7, r.gate_hbm.at[0], r.gate),
         load(8, r.up_hbm.at[0], r.up),
         load(9, r.down_hbm.at[0], r.down.at[0]),
     ]
-    go("swap", 0, r.down_hbm.at[0], r.down.at[1], partner)
-
-    for i in range(1, 8):
-        arrived("t1", i, r.table1.at[:, (p - i + 8) % 8], across(8 - i))
+    go(("swap", 0), ("swap", 0), r.down_hbm.at[0], r.down.at[1], partner)
+
+    arrived("t1", 0, r.table1.at[:, pl.ds(0, 7)], partner)
     r.table2[:, c] = r.table1[...]
     for j in range(1, 8):
-        go("t2", j, r.table1, r.table2.at[:, c], along(j))
+        go(("t2", 0), ("t2", 0), r.table1, r.table2.at[:, c], along(j))
 
     for j in range(8):
         columns = slice(j * 128, j * 128 + 128)
@@ -280,35 +297,34 @@
             r.attended[side, :, h * 128 : h * 128 + 128] = result[start : start + 64]
 
     def gathered(b, side):
-        return r.selected.at[pl.ds(b * 64, 64), pl.ds(pl.multiple_of(side * 384, 128), 384)]
-
-    own_rows = pltpu.make_async_copy(r.attended.at[k], gathered(c, k), r.att_r.at[0, 0])
+        start = pl.multiple_of(b * 64, 64)
+        return r.selected.at[pl.ds(start, 64), pl.ds(pl.multiple_of(side * 384, 128), 384)]
+
+    part_of = c // 4
+    own_rows = pltpu.make_async_copy(r.attended.at[k], gathered(c, k), r.att_r.at[part_of])
     own_rows.start()
     for j in range(8):
         if j > 0:
-            go("att", (j, 0), r.attended.at[k], gathered(c, k), along(j))
-        go("att", (j, 1), r.attended.at[1 - k], gathered(c, k), along_other(j))
-
-    for j in range(1, 8):
-        arrived("t2", j, r.table2.at[:, (c - j + 8) % 8], along(8 - j))
+            go(("att", 0), ("att", part_of), r.attended.at[k], gathered(c, k), along(j))
+        go(("att", 0), ("att", part_of), r.attended.at[1 - k], gathered(c, k), along_other(j))
+
+    arrived("t2", 0, r.table2.at[:, pl.ds(0, 7)], partner)
     r.tables[k] = r.table2[k]
-    go("t3", 0, r.table2.at[1 - k], r.tables.at[k], partner)
+    go(("t3", 0), ("t3", 0), r.table2.at[1 - k], r.tables.at[k], partner)
 
     own_weight.wait()
     arrived("weight", 0, out_weight(1 - k), partner)
 
     def partial(i, part):
-        return r.selected.at[pl.ds((i * 2 + part) * 32, 32), pl.ds(2304, 768)]
+        return r.selected.at[pl.ds((part * 8 + i) * 32, 32), pl.ds(2304, 768)]
 
     for part in range(2):
-        for b in range(part * 4, part * 4 + 4):
-            j = (c - b + 8) % 8
-            arrived("att", (j, 0), gathered(b, k), partner)
-            arrived("att", (j, 1), gathered(b, 1 - k), partner)
+        rows_of = slice(part * 256, part * 256 + 256)
+        arrived("att", part, r.selected.at[pl.ds(part * 256, 256), pl.ds(0, 768)], partner)
         value = None
         for side in range(2):
             term = jnp.dot(
-                r.selected[part * 256 : part * 256 + 256, side * 384 : side * 384 + 384],
+                r.selected[rows_of, side * 384 : side * 384 + 384],
                 r.selected[0:384, 768 + side * 768 : 1536 + side * 768],
                 preferred_element_type=F32,
             )
@@ -318,30 +334,34 @@
                 [value[b * 64 + i * 8 : b * 64 + i * 8 + 8] for b in range(4)], axis=0
             ).astype(BF16)
         for i in range(1, 8):
-            go("sum", (i, part), partial((p + i) % 8, part), r.partial_in.at[i, part], across(i))
+            go(
+                ("sum", 0),
+                ("sum", part),
+                partial((p + i) % 8, part),
+                r.partial_in.at[part, i],
+                across(i),
+            )
     for part in range(2):
         value = partial(p, part)[...].astype(F32)
+        arrived("sum", part, r.partial_in.at[part, pl.ds(1, 7)], partner)
         for i in range(1, 8):
-            arrived("sum", (i, part), r.partial_in.at[i, part], across(8 - i))
-            value = value + r.partial_in[i, part].astype(F32)
+            value = value + r.partial_in[part, i].astype(F32)
         r.summed[part * 4 : part * 4 + 4] = value.reshape(4, 8, 768)
     r.summed_in[c] = r.summed[c]
     for j in range(1, 8):
-        go("back", j, r.summed.at[(c + j) % 8], r.summed_in.at[c], along(j))
-    for j in range(1, 8):
-        arrived("back", j, r.summed_in.at[(c - j + 8) % 8], along(8 - j))
+        go(("back", 0), ("back", 0), r.summed.at[(c + j) % 8], r.summed_in.at[c], along(j))
+    loads[4].wait()
+    loads[5].wait()
+    arrived("back", 0, r.summed_in.at[pl.ds(0, 7)], partner)
     for b in range(8):
         columns = slice(b * 768, b * 768 + 768)
-        if b == 0:
-            loads[4].wait()
-            loads[5].wait()
         r.hidden[:, columns] = r.residual[:, columns].astype(F32) + r.summed_in[b]
     hidden = r.hidden[...]
     centered = hidden - jnp.mean(hidden, axis=1, keepdims=True)
     variance = jnp.mean(centered * centered, axis=1, keepdims=True)
     normed = centered * lax.rsqrt(variance + 1e-05) * r.gain[...]
 
-    links.settle()
+    left("sum", 0, r.partial_in.at[:, pl.ds(0, 7)], partner)
 
     def ring(axis, by):
         return (at[axis] + by + 4) % 4
@@ -369,7 +389,7 @@
                 [normed[:, low : low + 512], normed[:, high : high + 512]], axis=0
             ).astype(BF16)
         for d in (1, -1, 2):
-            go("ag1", (q, d % 4), piece(q, 0), piece(q, 0), near[ORDERS[q][0], d])
+            go(("ag1", 0), ("ag1", q), piece(q, 0), piece(q, 0), near[ORDERS[q][0], d])
 
     arrived("t3", 0, r.tables.at[1 - k], partner)
     tables = r.tables[...].reshape(128, 128)
@@ -422,32 +442,34 @@
 
     def forward(q, s, d, g):
         region = group(q, s, d, g)
-        go("fwd", (q, s, d % 4, g % 4), region, region, partner)
+        go(("fwd", 0), ("fwd", (q, s)), region, region, partner)
 
     def ring_send(q, s, g):
         for kind, d in ((0, 1), (1, -1)):
             region = group(q, s, 0, g)
-            go("ag3", (q, s, g % 4, kind), region, region, near[ORDERS[q][2], d])
+            go(("ag3", 0), ("ag3", (q, s, g % 4, kind)), region, region, near[ORDERS[q][2], d])
 
     def ring_relay(q, s, g):
         for kind, d in ((0, 1), (1, -1)):
             whole = group(q, s, -d, g)
             arrived("ag3", (q, s, g % 4, kind), whole, near[ORDERS[q][2], -d])
             part = half(whole, kind)
-            go("ag3", (q, s, g % 4, 2 + kind), part, part, near[ORDERS[q][2], d])
+            go(("ag3", 0), ("ag3end", (q, s, kind)), part, part, near[ORDERS[q][2], d])
             forward(q, s, -d, g)
 
-    def ring_finish(q, s, g):
+    def ring_finish(q, s):
+        a1, a2, a3 = ORDERS[q]
         for kind, d in ((0, 1), (1, -1)):
-            part = half(group(q, s, 2, g), kind)
-            arrived("ag3", (q, s, g % 4, 2 + kind), part, near[ORDERS[q][2], -d])
-        forward(q, s, 2, g)
-
-    for q in range(3):
+            part = r.rows.at[k, q, ring(a3, 2), :, pl.ds(kind * 2, 2), s]
+            arrived("ag3end", (q, s, kind), part, near[a3, -d])
+        for g in OFFSETS:
+            forward(q, s, 2, g)
+
+    for q in range(3):
+        a1, a2, a3 = ORDERS[q]
+        arrived("ag1", q, r.rows.at[k, q, at[a3], at[a2], pl.ds(0, 3)], near[a1, 1])
         for d in (1, -1, 2):
-            arrived("ag1", (q, d % 4), piece(q, -d), near[ORDERS[q][0], -d])
-        for d in (1, -1, 2):
-            go("ag2", (q, d % 4), line(q, 0), line(q, 0), near[ORDERS[q][1], d])
+            go(("ag2", 0), ("ag2", (q, d % 4)), line(q, 0), line(q, 0), near[a2, d])
         ring_send(q, 0, 0)
         for s in range(2):
             forward(q, s, 0, 0)
@@ -463,18 +485,15 @@
     for g in OFFSETS:
         for q in range(3):
             ring_relay(q, 0, g)
-            ring_send(q, 1, g)
     for g in OFFSETS:
         for q in range(3):
-            ring_finish(q, 0, g)
+            ring_send(q, 1, g)
+    for q in range(3):
+        ring_finish(q, 0)
 
     def select(s):
         for q in range(3):
-            for d in OFFSETS:
-                for g in OFFSETS:
-                    arrived(
-                        "fwd", (q, s, d % 4, g % 4), group(q, s, d, g, 1 - k), partner
-                    )
+            arrived("fwd", (q, s), r.rows.at[1 - k, q, :, :, :, s], partner)
         slots = lax.broadcasted_iota(jnp.int32, (256, 512), 0).astype(F32)
         for z in range(4):
             for q in range(3):
@@ -523,9 +542,8 @@
     r.sums[:, 768:1440] = product(r.up, 0)
     for q in range(3):
         ring_relay(q, 1, 2)
-    for g in OFFSETS:
-        for q in range(3):
-            ring_finish(q, 1, g)
+    for q in range(3):
+        ring_finish(q, 1)
     select(1)
     r.sums[:, 0:672] += product(r.gate, 1)
     r.sums[:, 768:1440] += product(r.up, 1)
@@ -542,17 +560,17 @@
         r.mixed[0, block] = value[:128].astype(BF16)
         r.mixed[1, block] = value[128:].astype(BF16)
         go(
-            "mix",
-            z,
+            ("mix", 0),
+            ("mix", 0),
             r.mixed.at[1 - k, pl.ds(z * 128, 128)],
             r.mixed_other.at[pl.ds(z * 128, 128)],
             partner,
         )
     big_loads[2].wait()
-    arrived("swap", 0, r.down.at[1], partner)
-    for z in range(4):
-        arrived("mix", z, r.mixed_other.at[pl.ds(z * 128, 128)], partner)
-    links.settle()
+    left("ag1", 0, r.rows.at[k, :, pl.ds(0, 3), 0, 0], partner)
+    left("ag2", 0, r.rows.at[k, :, pl.ds(0, 3), 0], partner)
+    left("ag3", 0, r.rows.at[k, :, pl.ds(0, 3)], partner)
+    left("fwd", 0, r.rows.at[k], partner)
 
     def down_unit(q, s):
         sides = []
@@ -560,7 +578,11 @@
             start = column_of(h, s, q)
             value = jnp.dot(
                 r.mixed[k], r.down[0, :, start : start + 512], preferred_element_type=F32
-            ) + jnp.dot(
+            )
+            if (q, s, h) == (0, 0, 0):
+                arrived("mix", 0, r.mixed_other, partner)
+                arrived("swap", 0, r.down.at[1], partner)
+            value = value + jnp.dot(
                 r.mixed_other[...], r.down[1, :, start : start + 512], preferred_element_type=F32
             )
             sides.append(value.reshape(64, 8, 512))
@@ -585,8 +607,8 @@
         for g in GROUPS_BACK:
             for kind, d in ((0, 1), (1, -1)):
                 go(
-                    "rs3",
-                    (q, s, g % 4, kind),
+                    ("rs3", 0),
+                    ("rs3", (q, s, g % 4, kind)),
                     half(group(q, s, 2, g), kind),
                     r.relay3.at[q, s, g % 4, kind],
                     near[ORDERS[q][2], d],
@@ -600,8 +622,8 @@
                 whole = group(q, s, d, g)
                 add_into(half(whole, kind), slot)
                 go(
-                    "rs3",
-                    (q, s, g % 4, 2 + kind),
+                    ("rs3", 0),
+                    ("rs3end", (q, s, g % 4)),
                     whole,
                     r.full3.at[q, s, g % 4, kind],
                     near[ORDERS[q][2], d],
@@ -609,33 +631,31 @@
 
     def back_third(q, s, g):
         slots = [r.full3.at[q, s, g % 4, kind] for kind in range(2)]
-        for kind, d in ((0, 1), (1, -1)):
-            arrived("rs3", (q, s, g % 4, 2 + kind), slots[kind], near[ORDERS[q][2], -d])
+        arrived("rs3end", (q, s, g % 4), r.full3.at[q, s, g % 4], partner)
         whole = group(q, s, 0, g)
         add_into(whole, *slots)
         if g != 0:
-            go("rs2", (q, s, g % 4), whole, r.full2.at[q, s, g % 4], near[ORDERS[q][1], g])
+            slot = r.full2.at[q, s, g % 4]
+            go(("rs2", 0), ("rs2", (q, s)), whole, slot, near[ORDERS[q][1], g])
 
     def back_line(q, s):
         slots = [r.full2.at[q, s, g % 4] for g in (1, -1, 2)]
-        for g, slot in zip((1, -1, 2), slots, strict=True):
-            arrived("rs2", (q, s, g % 4), slot, near[ORDERS[q][1], -g])
+        arrived("rs2", (q, s), r.full2.at[q, s, pl.ds(1, 3)], partner)
         add_into(group(q, s, 0, 0), *slots)
         for d in (1, -1, 2):
             go(
-                "rs1",
-                (q, s, d % 4),
+                ("rs1", 0),
+                ("rs1", (q, s)),
                 piece(q, d).at[s],
                 r.full1.at[q, s, d % 4],
                 near[ORDERS[q][0], d],
             )
 
     def back_end(q, s):
+        arrived("rs1", (q, s), r.full1.at[q, s, pl.ds(1, 3)], partner)
         value = piece(q, 0)[s].astype(F32)
         for d in (1, -1, 2):
-            slot = r.full1.at[q, s, d % 4]
-            arrived("rs1", (q, s, d % 4), slot, near[ORDERS[q][0], -d])
-            value = value + slot[...].astype(F32)
+            value = value + r.full1[q, s, d % 4].astype(F32)
         for h in range(2):
             start = column_of(h, s, q)
             columns = slice(start, start + 512)
@@ -661,17 +681,27 @@
         for q in range(3):
             back_end(q, s)
 
-    links.settle()
+    left("rs3", 0, r.rows.at[k, :, pl.ds(0, 3)], partner)
+    left("rs2", 0, r.rows.at[k, :, pl.ds(0, 3), 0], partner)
+    left("rs1", 0, r.rows.at[k, :, pl.ds(0, 3), 0, 0], partner)
+    left("mix", 0, r.mixed_other, partner)
+    left("swap", 0, r.down.at[1], partner)
+    left("weight", 0, r.weight_hbm, partner)
+    left("t1", 0, r.table1.at[:, pl.ds(0, 7)], partner)
+    left("t2", 0, r.table2.at[:, pl.ds(0, 7)], partner)
+    left("t3", 0, r.table2.at[0], partner)
+    left("pair", 0, own_block, partner)
+    left("att", 0, r.selected.at[pl.ds(0, 480), pl.ds(0, 768)], partner)
+    left("back", 0, r.summed.at[pl.ds(0, 7)], partner)
     for j in range(1, 8):
 
         @pl.when(c + j < 8)
         def _(j=j):
-            links.copy("kv", j, own_block, own_block, along(j)).wait_send()
+            left("kv", j, own_block, along(j))
 
         @pl.when(c - j >= 0)
         def _(j=j):
-            region = r.blocks.at[c - j, k]
-            links.copy("pair", j, region, region, partner).wait_send()
+            left("pair", j, r.blocks.at[c - j, k], partner)
 
 
 def on_device(
@@ -687,8 +717,8 @@
     down_weight,
 ):
     scratch = [pltpu.VMEM(shape, kind) for shape, kind in SCRATCH.values()]
-    for shape in SEMAPHORES.values():
-        scratch += [pltpu.SemaphoreType.DMA(shape)] * 2
+    for shape in [*SENDS.values(), *RECEIVES.values()]:
+        scratch.append(pltpu.SemaphoreType.DMA(shape))
     return pl.pallas_call(
         layer_kernel,
         name="layer",

time: 140 us -> 134 us (0.957)
  Pallas kernels: 138 us -> 132 us
    pallas_call x1, Pallas kernels: 138 us -> 132 us  [on_device(): pl.pallas_call(layer_kernel, name='layer', out_shape=jax.ShapeDtypeStruct...]
where the time goes in v3:
time: 134 us; the launch traced here: 133 us
  Pallas kernels  132 us (99%)
  local copies, waits for them, and re-layouts  1.54 us (1%)
    pallas_call x1, Pallas kernels, on_device(): pl.pallas_call(layer_kernel, name='layer', out_shape=jax.ShapeDtypeStruct...  132 us

profile of v3, /device:TPU:0, one launch (start us, length us, event | category | flops | bytes accessed | tf_op | source)
XLA Modules:
  0.0 133.5 jit_solution(13412412116598357685)
XLA Ops:
  0.0 131.9 %layer.1 = bf16[8,6144]{1,0:T(8,128)(2,1)} custom-call(bf16[128,384]{1,0:T(8,128)(2,1)} %refs_0_.1, bf16[2,64,128]{2,1,0:T(8,128)(2,1)} %bitcast.8, bf16[8,6144]{1,0:T(8,128)(2,1)} %refs_2_.1, f32[1,6144]{1,0:T(1,128)} %bitcast.9, s32[4,8]{1,0:T(4,128)} %bitcast.10, f32[4,8]{1,0:T(4,128)} %bitcast.11, bf16[384,768]{1,0:T(8,128)(2,1)} %refs_6_.1, ...), custom_call_target="tpu_custom_call" | custom-call | tf_op jit(solution)/shard_map/layer/pallas_call | solution.py:722
  131.9 1.5 %copy.12 = bf16[8,6144]{1,0:T(8,128)(2,1)} copy(bf16[8,6144]{1,0:T(8,128)(2,1)} %layer.1) | data formatting | bytes 196608

commit v4 on v3

--- a/solution.py
+++ b/solution.py
@@ -14,7 +14,8 @@
 F32 = jnp.float32
 ORDERS = (("x", "y", "z"), ("y", "z", "x"), ("z", "x", "y"))
 OFFSETS = (0, -1, 1, 2)
-GROUPS_BACK = (2, 1, -1, 0)
+ROUNDS = 4
+WIDTH = 3072 // 3 // ROUNDS
 
 SCRATCH = {
     "query": ((128, 384), BF16),
@@ -33,14 +34,15 @@
     "table2": ((2, 8, 8, 1, 128), F32),
     "tables": ((2, 8, 8, 1, 128), F32),
     "targets": ((8, 1, 512), F32),
+    "spread": ((2, 4, 256, 128), BF16),
     "gate": ((672, 6144), BF16),
     "up": ((672, 6144), BF16),
     "down": ((2, 672, 6144), BF16),
-    "rows": ((2, 3, 4, 4, 4, 2, 16, 512), BF16),
-    "relay3": ((3, 2, 4, 2, 2, 16, 512), BF16),
-    "full3": ((3, 2, 4, 2, 4, 16, 512), BF16),
-    "full2": ((3, 2, 4, 4, 16, 512), BF16),
-    "full1": ((3, 2, 4, 16, 512), BF16),
+    "rows": ((2, 3, 4, 4, 4, ROUNDS, 16, WIDTH), BF16),
+    "relay3": ((3, ROUNDS, 2, 2, 4, 16, WIDTH), BF16),
+    "full3": ((3, ROUNDS, 2, 4, 4, 16, WIDTH), BF16),
+    "full2": ((3, ROUNDS, 4, 4, 16, WIDTH), BF16),
+    "full1": ((3, ROUNDS, 4, 16, WIDTH), BF16),
     "selected": ((512, 3072), BF16),
     "sums": ((512, 1536), F32),
     "mixed": ((2, 512, 672), BF16),
@@ -79,15 +81,16 @@
     "t3": (1,),
     "ag1": (3,),
     "ag2": (3, 4),
-    "ag3": (3, 2, 4, 2),
-    "ag3end": (3, 2, 2),
-    "fwd": (3, 2),
+    "ag3": (3, ROUNDS, 4, 2),
+    "ag3end": (3, ROUNDS, 2),
+    "fwd": (3, ROUNDS),
+    "fwd0": (3,),
     "swap": (1,),
     "mix": (1,),
-    "rs3": (3, 2, 4, 2),
-    "rs3end": (3, 2, 4),
-    "rs2": (3, 2),
-    "rs1": (3, 2),
+    "rs3": (3, ROUNDS, 2),
+    "rs3end": (3, ROUNDS),
+    "rs2": (3, ROUNDS),
+    "rs1": (3, ROUNDS),
 }
 INPUTS = (
     "query_hbm",
@@ -114,7 +117,7 @@
 
 
 def column_of(h, s, q):
-    return h * 3072 + s * 1536 + q * 512
+    return h * 3072 + (s * 3 + q) * WIDTH
 
 
 class Links:
@@ -341,6 +344,65 @@
                 r.partial_in.at[part, i],
                 across(i),
             )
+    arrived("t3", 0, r.tables.at[1 - k], partner)
+    tables = r.tables[...].reshape(128, 128)
+    table_high = tables.astype(BF16)
+    table_low = (tables - table_high.astype(F32)).astype(BF16)
+
+    def table_rows(turn, z):
+        row = lax.broadcasted_iota(jnp.int32, (32, 128), 0)
+        slow, fast = row // 4 % 4, row % 4
+        x, y = (slow, fast) if turn else (fast, slow)
+        source = row // 16 * 64 + z * 16 + x % 2 * 8 + y * 2 + x // 2
+        wanted = source == lax.broadcasted_iota(jnp.int32, (32, 128), 1)
+        chooser = jnp.where(wanted, 1.0, 0.0).astype(BF16)
+        return jnp.dot(chooser, table_high, preferred_element_type=F32) + jnp.dot(
+            chooser, table_low, preferred_element_type=F32
+        )
+
+    def pick_targets(turn, z):
+        codes = table_rows(turn, z)[:, :8].astype(BF16)
+        tile = lax.broadcasted_iota(jnp.int32, (8, 512), 1) % 8
+        repeat = jnp.where(tile == lax.broadcasted_iota(jnp.int32, (8, 512), 0), 1.0, 0.0)
+        spread = jnp.dot(codes, repeat.astype(BF16), preferred_element_type=F32)
+        column = lax.broadcasted_iota(jnp.int32, (32, 512), 1)
+        own = column // 16 == lax.broadcasted_iota(jnp.int32, (32, 512), 0)
+        code = jnp.sum(jnp.where(own, spread, 0.0), axis=0, keepdims=True)
+        column = lax.broadcasted_iota(jnp.int32, (1, 512), 1)
+        chip = column // 16 % 16
+        if turn:
+            chip = chip % 4 * 4 + chip // 4
+        base = column // 8 % 2 * 128 + chip * 8 + column // 256 * 4 - 1
+        return jnp.where(code > 0, base.astype(F32) + code, -1.0)
+
+    def slot_columns(z):
+        found = table_rows(0, z)
+        row = lax.broadcasted_iota(jnp.int32, (256, 32), 0)
+        repeat = jnp.where(row // 8 == lax.broadcasted_iota(jnp.int32, (256, 32), 1), 1.0, 0.0)
+        repeat = repeat.astype(BF16)
+        high = found.astype(BF16)
+        low = (found - high.astype(F32)).astype(BF16)
+        spread = jnp.dot(repeat, high, preferred_element_type=F32) + jnp.dot(
+            repeat, low, preferred_element_type=F32
+        )
+        lane = lax.broadcasted_iota(jnp.int32, (256, 128), 1)
+        row = lax.broadcasted_iota(jnp.int32, (256, 128), 0)
+        code = jnp.sum(jnp.where(lane == row % 8, spread, 0.0), axis=1, keepdims=True)
+        share = jnp.sum(jnp.where(lane == row % 8 + 8, spread, 0.0), axis=1, keepdims=True)
+        row = lax.broadcasted_iota(jnp.int32, (256, 1), 0)
+        base = row // 8 % 16 * 8 + row // 128 * 4 - 1
+        return jnp.where(code > 0, base.astype(F32) + code, -1.0), share
+
+    for z in range(4):
+        for turn in range(2):
+            r.targets[turn * 4 + z] = pick_targets(turn, z)
+    number = lax.broadcasted_iota(jnp.int32, (256, 128), 1).astype(F32)
+    for z in range(4):
+        place_of, share = slot_columns(z)
+        spread = jnp.where(number == place_of, share, 0.0)
+        r.spread[0, z] = spread.astype(BF16)
+        r.spread[1, z] = (spread - r.spread[0, z].astype(F32)).astype(BF16)
+
     for part in range(2):
         value = partial(p, part)[...].astype(F32)
         arrived("sum", part, r.partial_in.at[part, pl.ds(1, 7)], partner)
@@ -383,66 +445,22 @@
         return ref.at[pl.ds(index * 2, 2)]
 
     for q in range(3):
-        for s in range(2):
+        for s in range(ROUNDS):
             low, high = column_of(0, s, q), column_of(1, s, q)
             piece(q, 0)[s] = jnp.concatenate(
-                [normed[:, low : low + 512], normed[:, high : high + 512]], axis=0
+                [normed[:, low : low + WIDTH], normed[:, high : high + WIDTH]], axis=0
             ).astype(BF16)
         for d in (1, -1, 2):
             go(("ag1", 0), ("ag1", q), piece(q, 0), piece(q, 0), near[ORDERS[q][0], d])
 
-    arrived("t3", 0, r.tables.at[1 - k], partner)
-    tables = r.tables[...].reshape(128, 128)
-    table_high = tables.astype(BF16)
-    table_low = (tables - table_high.astype(F32)).astype(BF16)
-
-    def table_rows(turn, z):
-        row = lax.broadcasted_iota(jnp.int32, (32, 128), 0)
-        slow, fast = row // 4 % 4, row % 4
-        x, y = (slow, fast) if turn else (fast, slow)
-        source = row // 16 * 64 + z * 16 + x % 2 * 8 + y * 2 + x // 2
-        wanted = source == lax.broadcasted_iota(jnp.int32, (32, 128), 1)
-        chooser = jnp.where(wanted, 1.0, 0.0).astype(BF16)
-        return jnp.dot(chooser, table_high, preferred_element_type=F32) + jnp.dot(
-            chooser, table_low, preferred_element_type=F32
-        )
-
-    def pick_targets(turn, z):
-        codes = table_rows(turn, z)[:, :8].astype(BF16)
-        tile = lax.broadcasted_iota(jnp.int32, (8, 512), 1) % 8
-        repeat = jnp.where(tile == lax.broadcasted_iota(jnp.int32, (8, 512), 0), 1.0, 0.0)
-        spread = jnp.dot(codes, repeat.astype(BF16), preferred_element_type=F32)
-        column = lax.broadcasted_iota(jnp.int32, (32, 512), 1)
-        own = column // 16 == lax.broadcasted_iota(jnp.int32, (32, 512), 0)
-        code = jnp.sum(jnp.where(own, spread, 0.0), axis=0, keepdims=True)
-        column = lax.broadcasted_iota(jnp.int32, (1, 512), 1)
-        chip = column // 16 % 16
-        if turn:
-            chip = chip % 4 * 4 + chip // 4
-        base = column // 8 % 2 * 128 + chip * 8 + column // 256 * 4 - 1
-        return jnp.where(code > 0, base.astype(F32) + code, -1.0)
-
-    def slot_columns(z):
-        found = table_rows(0, z)
-        row = lax.broadcasted_iota(jnp.int32, (256, 32), 0)
-        repeat = jnp.where(row // 8 == lax.broadcasted_iota(jnp.int32, (256, 32), 1), 1.0, 0.0)
-        repeat = repeat.astype(BF16)
-        high = found.astype(BF16)
-        low = (found - high.astype(F32)).astype(BF16)
-        spread = jnp.dot(repeat, high, preferred_element_type=F32) + jnp.dot(
-            repeat, low, preferred_element_type=F32
-        )
-        lane = lax.broadcasted_iota(jnp.int32, (256, 128), 1)
-        row = lax.broadcasted_iota(jnp.int32, (256, 128), 0)
-        code = jnp.sum(jnp.where(lane == row % 8, spread, 0.0), axis=1, keepdims=True)
-        share = jnp.sum(jnp.where(lane == row % 8 + 8, spread, 0.0), axis=1, keepdims=True)
-        row = lax.broadcasted_iota(jnp.int32, (256, 1), 0)
-        base = row // 8 % 16 * 8 + row // 128 * 4 - 1
-        return jnp.where(code > 0, base.astype(F32) + code, -1.0), share
-
-    def forward(q, s, d, g):
-        region = group(q, s, d, g)
-        go(("fwd", 0), ("fwd", (q, s)), region, region, partner)
+    def plane(q, s, d):
+        return r.rows.at[k, q, ring(ORDERS[q][2], d), :, :, s]
+
+    def forward(q, s, d):
+        go(("fwd", 0), ("fwd", (q, s)), plane(q, s, d), plane(q, s, d), partner)
+
+    def forward_own(q, g):
+        go(("fwd", 0), ("fwd0", q), line(q, g), line(q, g), partner)
 
     def ring_send(q, s, g):
         for kind, d in ((0, 1), (1, -1)):
@@ -455,15 +473,31 @@
             arrived("ag3", (q, s, g % 4, kind), whole, near[ORDERS[q][2], -d])
             part = half(whole, kind)
             go(("ag3", 0), ("ag3end", (q, s, kind)), part, part, near[ORDERS[q][2], d])
-            forward(q, s, -d, g)
+            if g == 2:
+                forward(q, s, -d)
+
+    def plane_send(q, s):
+        for kind, d in ((0, 1), (1, -1)):
+            whole = plane(q, s, 0)
+            go(("ag3", 0), ("ag3", (q, s, 0, kind)), whole, whole, near[ORDERS[q][2], d])
+
+    def plane_relay(q, s):
+        for kind, d in ((0, 1), (1, -1)):
+            whole = plane(q, s, -d)
+            arrived("ag3", (q, s, 0, kind), whole, near[ORDERS[q][2], -d])
+            part = half(whole, kind)
+            go(("ag3", 0), ("ag3end", (q, s, kind)), part, part, near[ORDERS[q][2], d])
+            forward(q, s, -d)
 
     def ring_finish(q, s):
         a1, a2, a3 = ORDERS[q]
         for kind, d in ((0, 1), (1, -1)):
-            part = r.rows.at[k, q, ring(a3, 2), :, pl.ds(kind * 2, 2), s]
+            if s == 0:
+                part = r.rows.at[k, q, ring(a3, 2), :, pl.ds(kind * 2, 2), s]
+            else:
+                part = half(plane(q, s, 2), kind)
             arrived("ag3end", (q, s, kind), part, near[a3, -d])
-        for g in OFFSETS:
-            forward(q, s, 2, g)
+        forward(q, s, 2)
 
     for q in range(3):
         a1, a2, a3 = ORDERS[q]
@@ -471,29 +505,30 @@
         for d in (1, -1, 2):
             go(("ag2", 0), ("ag2", (q, d % 4)), line(q, 0), line(q, 0), near[a2, d])
         ring_send(q, 0, 0)
-        for s in range(2):
-            forward(q, s, 0, 0)
-    for z in range(4):
-        for turn in range(2):
-            r.targets[turn * 4 + z] = pick_targets(turn, z)
+        forward_own(q, 0)
     for g in (-1, 1, 2):
         for q in range(3):
             arrived("ag2", (q, -g % 4), line(q, g), near[ORDERS[q][1], g])
             ring_send(q, 0, g)
-            for s in range(2):
-                forward(q, s, 0, g)
+            forward_own(q, g)
+    def sends(s):
+        if s < ROUNDS:
+            for q in range(3):
+                plane_send(q, s)
+
+    sends(1)
     for g in OFFSETS:
         for q in range(3):
             ring_relay(q, 0, g)
-    for g in OFFSETS:
-        for q in range(3):
-            ring_send(q, 1, g)
+    sends(2)
     for q in range(3):
         ring_finish(q, 0)
 
     def select(s):
         for q in range(3):
-            arrived("fwd", (q, s), r.rows.at[1 - k, q, :, :, :, s], partner)
+            if s == 0:
+                arrived("fwd0", q, r.rows.at[1 - k, q, 0], partner)
+            arrived("fwd", (q, s), r.rows.at[1 - k, q, pl.ds(0, 3), :, :, s], partner)
         slots = lax.broadcasted_iota(jnp.int32, (256, 512), 0).astype(F32)
         for z in range(4):
             for q in range(3):
@@ -505,15 +540,15 @@
                         r.rows[side, q, :, z, :, s],
                         r.rows[side, q, :, :, z, s],
                     )[q]
-                    sides.append(found.reshape(256, 512))
+                    sides.append(found.reshape(256, WIDTH))
                 value = jnp.dot(
                     picker.astype(BF16),
                     jnp.concatenate(sides, axis=0),
                     preferred_element_type=F32,
                 ).astype(BF16)
                 for h in range(2):
-                    start = h * 1536 + q * 512
-                    r.selected[z * 128 : z * 128 + 128, start : start + 512] = value[
+                    start = (h * 3 + q) * WIDTH
+                    r.selected[z * 128 : z * 128 + 128, start : start + WIDTH] = value[
                         h * 128 : h * 128 + 128
                     ]
 
@@ -522,41 +557,43 @@
         for h in range(2):
             start = column_of(h, s, 0)
             term = lax.dot_general(
-                r.selected[:, h * 1536 : h * 1536 + 1536],
-                weight[:, start : start + 1536],
+                r.selected[:, h * 3 * WIDTH : h * 3 * WIDTH + 3 * WIDTH],
+                weight[:, start : start + 3 * WIDTH],
                 (((1,), (1,)), ((), ())),
                 preferred_element_type=F32,
             )
             value = term if value is None else value + term
         return value
 
-    select(0)
-    for q in range(3):
-        ring_relay(q, 1, 0)
-    big_loads[0].wait()
-    r.sums[:, 0:672] = product(r.gate, 0)
-    for g in (-1, 1):
-        for q in range(3):
-            ring_relay(q, 1, g)
-    big_loads[1].wait()
-    r.sums[:, 768:1440] = product(r.up, 0)
-    for q in range(3):
-        ring_relay(q, 1, 2)
-    for q in range(3):
-        ring_finish(q, 1)
-    select(1)
-    r.sums[:, 0:672] += product(r.gate, 1)
-    r.sums[:, 768:1440] += product(r.up, 1)
-
-    number = lax.broadcasted_iota(jnp.int32, (256, 128), 1).astype(F32)
+    for s in range(ROUNDS):
+        later = s + 1 < ROUNDS
+        select(s)
+        if later:
+            for q in range(3):
+                plane_relay(q, s + 1)
+        sends(s + 3)
+        if s == 0:
+            big_loads[0].wait()
+            r.sums[:, 0:672] = product(r.gate, s)
+        else:
+            r.sums[:, 0:672] += product(r.gate, s)
+        if s == 0:
+            big_loads[1].wait()
+            r.sums[:, 768:1440] = product(r.up, s)
+        else:
+            r.sums[:, 768:1440] += product(r.up, s)
+        if later:
+            for q in range(3):
+                ring_finish(q, s + 1)
+
     for z in range(4):
         block = slice(z * 128, z * 128 + 128)
         g = r.sums[block, 0:672]
         u = r.sums[block, 768:1440]
         activated = (g / (1.0 + jnp.exp(-g)) * u).astype(BF16)
-        place_of, share = slot_columns(z)
-        spread = jnp.where(number == place_of, 1.0, 0.0).astype(BF16)
-        value = jnp.dot(spread, activated, preferred_element_type=F32) * share
+        value = jnp.dot(r.spread[0, z], activated, preferred_element_type=F32) + jnp.dot(
+            r.spread[1, z], activated, preferred_element_type=F32
+        )
         r.mixed[0, block] = value[:128].astype(BF16)
         r.mixed[1, block] = value[128:].astype(BF16)
         go(
@@ -577,16 +614,16 @@
         for h in range(2):
             start = column_of(h, s, q)
             value = jnp.dot(
-                r.mixed[k], r.down[0, :, start : start + 512], preferred_element_type=F32
+                r.mixed[k], r.down[0, :, start : start + WIDTH], preferred_element_type=F32
             )
             if (q, s, h) == (0, 0, 0):
                 arrived("mix", 0, r.mixed_other, partner)
                 arrived("swap", 0, r.down.at[1], partner)
             value = value + jnp.dot(
-                r.mixed_other[...], r.down[1, :, start : start + 512], preferred_element_type=F32
+                r.mixed_other[...], r.down[1, :, start : start + WIDTH], preferred_element_type=F32
             )
-            sides.append(value.reshape(64, 8, 512))
-        joined = jnp.concatenate(sides, axis=1).astype(BF16).reshape(4, 4, 4, 16, 512)
+            sides.append(value.reshape(64, 8, WIDTH))
+        joined = jnp.concatenate(sides, axis=1).astype(BF16).reshape(4, 4, 4, 16, WIDTH)
         if q == 0:
             r.rows[k, 0, :, :, :, s] = joined
         elif q == 1:
@@ -604,39 +641,26 @@
         ref[...] = value.astype(BF16)
 
     def back_first(q, s):
-        for g in GROUPS_BACK:
-            for kind, d in ((0, 1), (1, -1)):
-                go(
-                    ("rs3", 0),
-                    ("rs3", (q, s, g % 4, kind)),
-                    half(group(q, s, 2, g), kind),
-                    r.relay3.at[q, s, g % 4, kind],
-                    near[ORDERS[q][2], d],
-                )
+        for kind, d in ((0, 1), (1, -1)):
+            slot = r.relay3.at[q, s, kind]
+            part = half(plane(q, s, 2), kind)
+            go(("rs3", 0), ("rs3", (q, s, kind)), part, slot, near[ORDERS[q][2], d])
 
     def back_second(q, s):
-        for g in GROUPS_BACK:
-            for kind, d in ((0, 1), (1, -1)):
-                slot = r.relay3.at[q, s, g % 4, kind]
-                arrived("rs3", (q, s, g % 4, kind), slot, near[ORDERS[q][2], -d])
-                whole = group(q, s, d, g)
-                add_into(half(whole, kind), slot)
-                go(
-                    ("rs3", 0),
-                    ("rs3end", (q, s, g % 4)),
-                    whole,
-                    r.full3.at[q, s, g % 4, kind],
-                    near[ORDERS[q][2], d],
-                )
-
-    def back_third(q, s, g):
-        slots = [r.full3.at[q, s, g % 4, kind] for kind in range(2)]
-        arrived("rs3end", (q, s, g % 4), r.full3.at[q, s, g % 4], partner)
-        whole = group(q, s, 0, g)
-        add_into(whole, *slots)
-        if g != 0:
+        for kind, d in ((0, 1), (1, -1)):
+            slot = r.relay3.at[q, s, kind]
+            arrived("rs3", (q, s, kind), slot, near[ORDERS[q][2], -d])
+            whole = plane(q, s, d)
+            add_into(half(whole, kind), slot)
+            target = r.full3.at[q, s, kind]
+            go(("rs3", 0), ("rs3end", (q, s)), whole, target, near[ORDERS[q][2], d])
+
+    def back_third(q, s):
+        arrived("rs3end", (q, s), r.full3.at[q, s], partner)
+        add_into(plane(q, s, 0), r.full3.at[q, s, 0], r.full3.at[q, s, 1])
+        for g in (2, 1, -1):
             slot = r.full2.at[q, s, g % 4]
-            go(("rs2", 0), ("rs2", (q, s)), whole, slot, near[ORDERS[q][1], g])
+            go(("rs2", 0), ("rs2", (q, s)), group(q, s, 0, g), slot, near[ORDERS[q][1], g])
 
     def back_line(q, s):
         slots = [r.full2.at[q, s, g % 4] for g in (1, -1, 2)]
@@ -658,26 +682,23 @@
             value = value + r.full1[q, s, d % 4].astype(F32)
         for h in range(2):
             start = column_of(h, s, q)
-            columns = slice(start, start + 512)
+            columns = slice(start, start + WIDTH)
             r.out[:, columns] = (r.hidden[:, columns] + value[h * 8 : h * 8 + 8]).astype(BF16)
 
-    for q in range(3):
-        down_unit(q, 0)
-        back_first(q, 0)
-    for q in range(3):
-        down_unit(q, 1)
-        back_first(q, 1)
-        back_second(q, 0)
-    for q in range(3):
-        back_second(q, 1)
-    for s in range(2):
-        for g in GROUPS_BACK:
+    for s in range(ROUNDS + 2):
+        for q in range(3):
+            if s < ROUNDS:
+                down_unit(q, s)
+                back_first(q, s)
+            if 0 <= s - 1 < ROUNDS:
+                back_second(q, s - 1)
+        if s >= 2:
             for q in range(3):
-                back_third(q, s, g)
-    for s in range(2):
+                back_third(q, s - 2)
+    for s in range(ROUNDS):
         for q in range(3):
             back_line(q, s)
-    for s in range(2):
+    for s in range(ROUNDS):
         for q in range(3):
             back_end(q, s)
 

time: 134 us -> 132 us (0.985)
  Pallas kernels: 132 us -> 130 us
    pallas_call x1, Pallas kernels: 132 us -> 130 us  [on_device(): pl.pallas_call(layer_kernel, name='layer', out_shape=jax.ShapeDtypeStruct...]
where the time goes in v4:
time: 132 us
  Pallas kernels  130 us (98%)
  local copies, waits for them, and re-layouts  1.54 us (1%)
    pallas_call x1, Pallas kernels, on_device(): pl.pallas_call(layer_kernel, name='layer', out_shape=jax.ShapeDtypeStruct...  130 us

profile of v4, /device:TPU:0, one launch (start us, length us, event | category | flops | bytes accessed | tf_op | source)
XLA Modules:
  0.0 131.9 jit_solution(5587234731350828867)
XLA Ops:
  0.0 130.3 %layer.1 = bf16[8,6144]{1,0:T(8,128)(2,1)} custom-call(bf16[128,384]{1,0:T(8,128)(2,1)} %refs_0_.1, bf16[2,64,128]{2,1,0:T(8,128)(2,1)} %bitcast.8, bf16[8,6144]{1,0:T(8,128)(2,1)} %refs_2_.1, f32[1,6144]{1,0:T(1,128)} %bitcast.9, s32[4,8]{1,0:T(4,128)} %bitcast.10, f32[4,8]{1,0:T(4,128)} %bitcast.11, bf16[384,768]{1,0:T(8,128)(2,1)} %refs_6_.1, ...), custom_call_target="tpu_custom_call" | custom-call | tf_op jit(solution)/shard_map/layer/pallas_call | solution.py:743
  130.3 1.5 %copy.12 = bf16[8,6144]{1,0:T(8,128)(2,1)} copy(bf16[8,6144]{1,0:T(8,128)(2,1)} %layer.1) | data formatting | bytes 196608
